TPU v7x, 32 devices: a whole 2x2x4 slice. The times are simulated.
32 devices in a mesh: dp: 4 (over y, x), expert: 8 (over z, core).
Axes of the slice: x: 2, y: 2, z: 4, core: 2. Of those that a mesh axis runs over, the one named last changes fastest.
Arguments:
- tokens: bfloat16 [4096, 2048], P(('dp', 'expert')), may hold values from -6 to 6
- out_grad: bfloat16 [4096, 2048], P(('dp', 'expert')), may hold values from -6 to 6
- gate_probs: bfloat16 [4096, 4], P(('dp', 'expert')), may hold values from 0.049804688 to 0.59765625
- expert_ids: int32 [4096, 4], P(('dp', 'expert')), may hold values from 0 to 7, all different within a row; in each aligned block of 128 rows (0 to 127, 128 to 255, ...) at most 72 rows name the same one
- w_gate: bfloat16 [8, 2048, 768], P('expert'), may hold values from -0.125 to 0.125
- w_up: bfloat16 [8, 2048, 768], P('expert'), may hold values from -0.125 to 0.125
- w_down: bfloat16 [8, 768, 2048], P('expert'), may hold values from -0.21875 to 0.21875
Outputs:
- tokens_grad: bfloat16 [4096, 2048], P(('dp', 'expert'))
- probs_grad: float32 [4096, 4], P(('dp', 'expert'))
- gate_weight_grad: bfloat16 [8, 2048, 768], P('expert', None, 'dp')
- up_weight_grad: bfloat16 [8, 2048, 768], P('expert', None, 'dp')
- down_weight_grad: bfloat16 [8, 768, 2048], P('expert', 'dp')
Inputs may be any that keep to these rules, and one draw needn't show every extreme that they name: `expert_ids`: each row names 4 different experts. In each aligned block of 128 rows (the rows of one device) no expert is named by more than 72 rows, a bound that some block reaches.
All inputs are finite; a program needn't handle non-finite values.
Results may differ from a plain program's by a relative error of at most 0.0057.
Values may be sent and summed in bfloat16 or wider, within the bound.
A program may use at most 192 MiB of HBM per device.

v0:
```python
import jax
import jax.numpy as jnp
from jax import lax
from jax.sharding import PartitionSpec as P


def expert_work(x_slots, dy_slots, prob_slots, gate_mat, up_mat, down_mat):
    gate_pre = jnp.dot(x_slots, gate_mat, preferred_element_type=jnp.float32)
    up_pre = jnp.dot(x_slots, up_mat, preferred_element_type=jnp.float32)
    sigmoid_gate = jax.nn.sigmoid(gate_pre)
    silu_gate = gate_pre * sigmoid_gate
    hidden_act = silu_gate * up_pre
    hidden = hidden_act.astype(jnp.bfloat16)
    grad_hidden = lax.dot_general(
        dy_slots, down_mat, (((1,), (1,)), ((), ())), preferred_element_type=jnp.float32
    )
    prob_grad = jnp.sum(hidden_act * grad_hidden, axis=1)
    scaled_hidden = prob_slots[:, None] * grad_hidden
    grad_gate = (
        scaled_hidden * up_pre * sigmoid_gate * (1.0 + gate_pre * (1.0 - sigmoid_gate))
    ).astype(jnp.bfloat16)
    grad_up = (scaled_hidden * silu_gate).astype(jnp.bfloat16)
    scaled_dy = (prob_slots[:, None] * dy_slots.astype(jnp.float32)).astype(jnp.bfloat16)
    row_grad = lax.dot_general(
        grad_gate, gate_mat, (((1,), (1,)), ((), ())), preferred_element_type=jnp.float32
    )
    row_grad = row_grad + lax.dot_general(
        grad_up, up_mat, (((1,), (1,)), ((), ())), preferred_element_type=jnp.float32
    )
    return (hidden, grad_gate, grad_up, scaled_dy, row_grad, prob_grad)


def outer_rows(left, right):
    return lax.dot_general(
        left, right, (((0,), (0,)), ((), ())), preferred_element_type=jnp.float32
    )


def per_device(tokens, out_grad, gate_probs, expert_ids, w_gate, w_up, w_down):
    n_experts = lax.axis_size("expert")
    tok_rows, model_width = tokens.shape
    top_k = expert_ids.shape[1]
    capacity = tok_rows * top_k * 9 // (8 * n_experts)
    assigns = tok_rows * top_k
    flat_ids = expert_ids.reshape(assigns)
    onehot = (flat_ids[:, None] == jnp.arange(n_experts, dtype=jnp.int32)[None, :]).astype(
        jnp.int32
    )
    slot_rank = jnp.sum((jnp.cumsum(onehot, axis=0) - onehot) * onehot, axis=1)
    position = flat_ids * capacity + slot_rank
    table = (
        jnp.full((n_experts * capacity,), assigns, jnp.int32)
        .at[position]
        .set(jnp.arange(assigns, dtype=jnp.int32))
    )
    token_row = table // top_k
    tokens_pad = jnp.concatenate([tokens, jnp.zeros((1, model_width), jnp.bfloat16)], axis=0)
    grad_pad = jnp.concatenate([out_grad, jnp.zeros((1, model_width), jnp.bfloat16)], axis=0)
    probs_pad = jnp.concatenate(
        [gate_probs.reshape(assigns), jnp.zeros((1,), jnp.bfloat16)], axis=0
    )
    send_x = tokens_pad[token_row].reshape(n_experts, capacity, model_width)
    send_dy = grad_pad[token_row].reshape(n_experts, capacity, model_width)
    send_prob = probs_pad[table].reshape(n_experts, capacity)
    recv_x, recv_dy, recv_prob = (
        lax.all_to_all(send_x, "expert", split_axis=0, concat_axis=0, tiled=True),
        lax.all_to_all(send_dy, "expert", split_axis=0, concat_axis=0, tiled=True),
        lax.all_to_all(send_prob, "expert", split_axis=0, concat_axis=0, tiled=True),
    )
    slot_rows = n_experts * capacity
    x_slots = recv_x.reshape(slot_rows, model_width)
    dy_slots = recv_dy.reshape(slot_rows, model_width)
    prob_slots = recv_prob.reshape(slot_rows).astype(jnp.float32)
    gate_mat = w_gate[0]
    up_mat = w_up[0]
    down_mat = w_down[0]
    hidden, grad_gate, grad_up, scaled_dy, row_grad, prob_grad = expert_work(
        x_slots, dy_slots, prob_slots, gate_mat, up_mat, down_mat
    )
    back_rows, back_probs = (
        lax.all_to_all(
            row_grad.reshape(n_experts, capacity, model_width),
            "expert",
            split_axis=0,
            concat_axis=0,
            tiled=True,
        ),
        lax.all_to_all(
            prob_grad.reshape(n_experts, capacity),
            "expert",
            split_axis=0,
            concat_axis=0,
            tiled=True,
        ),
    )
    picked_rows = back_rows.reshape(slot_rows, model_width)[position]
    tokens_grad = jnp.sum(picked_rows.reshape(tok_rows, top_k, model_width), axis=1).astype(
        jnp.bfloat16
    )
    probs_grad = back_probs.reshape(slot_rows)[position].reshape(tok_rows, top_k)
    gate_term = outer_rows(x_slots, grad_gate)
    up_term = outer_rows(x_slots, grad_up)
    down_term = outer_rows(hidden, scaled_dy)
    gate_sum, up_sum, down_sum = (
        lax.psum_scatter(gate_term, "dp", scatter_dimension=1, tiled=True),
        lax.psum_scatter(up_term, "dp", scatter_dimension=1, tiled=True),
        lax.psum_scatter(down_term, "dp", scatter_dimension=0, tiled=True),
    )
    gate_weight_grad = gate_sum.astype(jnp.bfloat16)[None]
    up_weight_grad = up_sum.astype(jnp.bfloat16)[None]
    down_weight_grad = down_sum.astype(jnp.bfloat16)[None]
    return (tokens_grad, probs_grad, gate_weight_grad, up_weight_grad, down_weight_grad)


def solution(mesh):
    in_specs = (
        P(("dp", "expert"), None),
        P(("dp", "expert"), None),
        P(("dp", "expert"), None),
        P(("dp", "expert"), None),
        P("expert", None, None),
        P("expert", None, None),
        P("expert", None, None),
    )
    out_specs = (
        P(("dp", "expert"), None),
        P(("dp", "expert"), None),
        P("expert", None, "dp"),
        P("expert", None, "dp"),
        P("expert", "dp", None),
    )
    return jax.shard_map(
        per_device, mesh=mesh, in_specs=in_specs, out_specs=out_specs, check_vma=False
    )
```

profile of v0, /device:TPU:0, one launch (start us, length us, event | category | flops | bytes accessed | tf_op | source)
XLA Modules:
  0.0 387.0 jit_solution(17980961272173515990)
XLA Ops:
  10.3 1.1 reduce-window.6
  11.8 2.4 scatter_custom_fusion
  14.3 3.9 %gather_fusion = bf16[576]{0:T(1024)(128)(2,1)S(1)} fusion(bf16[513]{0:T(1024)(128)(2,1)S(1)} %pad_maximum_fusion, s32[1024]{0:T(1024)S(1)} %get-tuple-element.21), kind=kCustom, calls=%fused_computation | custom fusion | bytes 4608 | tf_op jit(solution)/shard_map/gather | solution.py:64
  19.0 6.3 %all-to-all-start = ((bf16[8,1,72]{2,1,0:T(2,128)(2,1)}), bf16[8,1,72]{2,1,0:T(2,128)(2,1)S(1)}, u32[]{:S(2)}, u32[]{:S(2)}) async-start(bf16[8,1,72]{2,1,0:T(2,128)(2,1)} %all_to_all.28), calls=%async_computation | async-start | bytes 8192 | tf_op jit(solution)/shard_map/all_to_all | solution.py:68
  25.3 1.9 concatenate.11
  27.2 7.9 %gather_fusion.2 = bf16[576,2048]{1,0:T(8,128)(2,1)} fusion(bf16[129,2048]{1,0:T(8,128)(2,1)} %concatenate.11, s32[1024]{0:T(1024)S(1)} %get-tuple-element.20), kind=kCustom, calls=%fused_computation.2 | custom fusion | bytes 4720896 | tf_op jit(solution)/shard_map/gather | solution.py:62
  35.1 5.1 %all-to-all-start.2 = ((bf16[8,72,2048]{2,1,0:T(8,128)(2,1)}), bf16[8,72,2048]{2,1,0:T(8,128)(2,1)}, u32[]{:S(2)}, u32[]{:S(2)}) async-start(bf16[8,72,2048]{2,1,0:T(8,128)(2,1)} %bitcast.50), calls=%async_computation.2 | async-start | bytes 4718592 | tf_op jit(solution)/shard_map/all_to_all | solution.py:66
  40.2 1.9 concatenate.10
  42.1 8.0 %gather_fusion.1 = bf16[576,2048]{1,0:T(8,128)(2,1)} fusion(bf16[129,2048]{1,0:T(8,128)(2,1)} %concatenate.10, s32[1024]{0:T(1024)S(1)} %get-tuple-element.20), kind=kCustom, calls=%fused_computation.1 | custom fusion | bytes 4720896 | tf_op jit(solution)/shard_map/gather | solution.py:63
  50.1 44.9 %all-to-all-done.2 = bf16[8,72,2048]{2,1,0:T(8,128)(2,1)} async-done(((bf16[8,72,2048]{2,1,0:T(8,128)(2,1)}), bf16[8,72,2048]{2,1,0:T(8,128)(2,1)}, u32[]{:S(2)}, u32[]{:S(2)}) %all-to-all-start.2) | async-done | bytes 2359328 | tf_op jit(solution)/shard_map/all_to_all | solution.py:66
  95.0 4.4 %all-to-all-start.1 = ((bf16[8,72,2048]{2,1,0:T(8,128)(2,1)}), bf16[8,72,2048]{2,1,0:T(8,128)(2,1)}, u32[]{:S(2)}, u32[]{:S(2)}) async-start(bf16[8,72,2048]{2,1,0:T(8,128)(2,1)} %bitcast.49), calls=%async_computation.1 | async-start | bytes 4718592 | tf_op jit(solution)/shard_map/all_to_all | solution.py:67
  99.8 5.0 %fusion.2 = f32[576,768]{1,0:T(8,128)} fusion(bf16[576,2048]{1,0:T(8,128)(2,1)} %bitcast.8, bf16[1,2048,768]{2,1,0:T(8,128)(2,1)S(1)} %copy-done), kind=kOutput, calls=%fused_computation.9 | convolution fusion | flops 1811939328 | bytes 7274496 | tf_op jit(solution)/shard_map/dot_general | solution.py:8
  104.8 4.9 %fusion.6 = f32[576,768]{1,0:T(8,128)} fusion(bf16[576,2048]{1,0:T(8,128)(2,1)} %bitcast.8, bf16[1,2048,768]{2,1,0:T(8,128)(2,1)S(1)} %copy-done.1), kind=kOutput, calls=%fused_computation.13 | convolution fusion | flops 1811939328 | bytes 7274496 | tf_op jit(solution)/shard_map/dot_general | solution.py:9
  109.7 44.4 %all-to-all-done.1 = bf16[8,72,2048]{2,1,0:T(8,128)(2,1)} async-done(((bf16[8,72,2048]{2,1,0:T(8,128)(2,1)}), bf16[8,72,2048]{2,1,0:T(8,128)(2,1)}, u32[]{:S(2)}, u32[]{:S(2)}) %all-to-all-start.1) | async-done | bytes 2359328 | tf_op jit(solution)/shard_map/all_to_all | solution.py:67
  154.1 8.2 %fusion.13 = f32[768,2048]{1,0:T(8,128)} fusion(bf16[576,2048]{1,0:T(8,128)(2,1)} %bitcast.5, f32[576]{0:T(1024)S(1)} %reshape.115, f32[576,768]{1,0:T(8,128)} %fusion.6, f32[576,768]{1,0:T(8,128)} %fusion.2), kind=kOutput, calls=%fused_computation.18 | convolution fusion | flops 1818132480 | bytes 12192000 | tf_op jit(solution)/shard_map/dot_general | solution.py:34
  162.4 7.2 %multiply_reduce_fusion = (f32[576]{0:T(1024)S(1)}, bf16[576,768]{1,0:T(8,128)(2,1)}, bf16[576,768]{1,0:T(8,128)(2,1)S(1)}) fusion(f32[576,768]{1,0:T(8,128)} %fusion.6, f32[576,768]{1,0:T(8,128)} %fusion.2, f32[576]{0:T(1024)S(1)} %reshape.115, bf16[576,2048]{1,0:T(8,128)(2,1)} %bitcast.5, bf16[1,768,2048]{2,1,0:T(8,128)(2,1)} %param.13), kind=kOutput, calls=%fused_computation.20 | convolution fusion | flops 1819459072 | bytes 10818048 | tf_op jit(solution)/shard_map/dot_general | solution.py:14
  169.6 0.9 copy-done.3
  170.5 6.2 %fusion.27 = f32[2048,768]{0,1:T(8,128)} fusion(bf16[576,2048]{1,0:T(8,128)(2,1)} %bitcast.8, bf16[576,768]{1,0:T(8,128)(2,1)S(1)} %get-tuple-element.17), kind=kOutput, calls=%fused_computation.56 | convolution fusion | flops 1811939328 | bytes 9535488 | tf_op jit(solution)/shard_map/dot_general | solution.py:34
  177.1 7.2 %fusion.26 = f32[2048,768]{0,1:T(8,128)} fusion(bf16[576,2048]{1,0:T(8,128)(2,1)} %bitcast.8, bf16[576,768]{1,0:T(8,128)(2,1)} %get-tuple-element.16), kind=kOutput, calls=%fused_computation.55 | convolution fusion | flops 1811939328 | bytes 9535488 | tf_op jit(solution)/shard_map/dot_general | solution.py:34
  184.9 3.3 all-to-all-start.4
  188.3 3.5 fusion
  191.8 4.3 %fusion.10 = f32[576,2048]{1,0:T(8,128)} fusion(f32[576,2048]{1,0:T(8,128)S(1)} %fusion, bf16[576,768]{1,0:T(8,128)(2,1)S(1)} %copy-done.4, bf16[1,2048,768]{2,1,0:T(8,128)(2,1)S(1)} %copy-done.2), kind=kOutput, calls=%fused_computation.17 | convolution fusion | flops 1813118976 | bytes 13467648 | tf_op jit(solution)/shard_map/dot_general | solution.py:27
  196.1 4.9 %all-to-all-start.3 = ((f32[8,72,2048]{2,1,0:T(8,128)}), f32[8,72,2048]{2,1,0:T(8,128)}, u32[]{:S(2)}, u32[]{:S(2)}) async-start(f32[8,72,2048]{2,1,0:T(8,128)} %bitcast.51), calls=%async_computation.3 | async-start | bytes 9437184 | tf_op jit(solution)/shard_map/all_to_all | solution.py:81
  202.2 2.3 gather_fusion.4
  205.3 101.0 %all-to-all-done.3 = f32[8,72,2048]{2,1,0:T(8,128)} async-done(((f32[8,72,2048]{2,1,0:T(8,128)}), f32[8,72,2048]{2,1,0:T(8,128)}, u32[]{:S(2)}, u32[]{:S(2)}) %all-to-all-start.3) | async-done | bytes 4718624 | tf_op jit(solution)/shard_map/all_to_all | solution.py:81
  306.3 7.8 %gather_fusion.3 = f32[512,2048]{1,0:T(8,128)} fusion(f32[576,2048]{1,0:T(8,128)} %bitcast.12, s32[1024]{0:T(1024)S(1)} %pad_clamp_fusion), kind=kCustom, calls=%fused_computation.3 | custom fusion | bytes 8390656 | tf_op jit(solution)/shard_map/gather | solution.py:96
  314.1 5.5 %reshape.112 = f32[128,4,2048]{2,1,0:T(4,128)} reshape(f32[512,2048]{1,0:T(8,128)} %gather_fusion.3) | data formatting | bytes 8388608 | tf_op jit(solution)/shard_map/reshape | solution.py:97
  319.6 5.7 %reduce_sum.31 = bf16[128,2048]{1,0:T(8,128)(2,1)} reduce(f32[128,4,2048]{2,1,0:T(4,128)} %reshape.112, f32[]{:T(128)} %constant.40.clone.1), dimensions={1}, to_apply=%region_4.5 | reduce | flops 786432 | bytes 4718596 | tf_op jit(solution)/shard_map/reduce_sum | solution.py:97
  325.3 2.4 convert_bitcast_fusion
  327.7 2.4 convert_bitcast_fusion.1
  330.1 48.0 %reduce-scatter.4.cloned.1.call-done = f32[2048,192]{0,1:T(8,128)} async-done(((f32[2048,768]{0,1:T(8,128)}), f32[2048,192]{0,1:T(8,128)}) %reduce-scatter.4.cloned.1.call-update) | async-done | bytes 1572880 | tf_op jit(solution)/shard_map/reduce_scatter | solution.py:105
  378.1 2.4 convert_bitcast_fusion.2
  (47 shorter events, 7.6 us)
Async XLA Ops:
  7.2 92.6 %copy-start = (bf16[1,2048,768]{2,1,0:T(8,128)(2,1)S(1)}, bf16[1,2048,768]{2,1,0:T(8,128)(2,1)}, u32[]{:S(2)}) copy-start(bf16[1,2048,768]{2,1,0:T(8,128)(2,1)} %param.11) | copy-start | bytes 9437188
  19.0 16.2 %all-to-all-start = ((bf16[8,1,72]{2,1,0:T(2,128)(2,1)}), bf16[8,1,72]{2,1,0:T(2,128)(2,1)S(1)}, u32[]{:S(2)}, u32[]{:S(2)}) async-start(bf16[8,1,72]{2,1,0:T(2,128)(2,1)} %all_to_all.28), calls=%async_computation | async-start | bytes 8192 | tf_op jit(solution)/shard_map/all_to_all | solution.py:68
  35.1 59.9 %all-to-all-start.2 = ((bf16[8,72,2048]{2,1,0:T(8,128)(2,1)}), bf16[8,72,2048]{2,1,0:T(8,128)(2,1)}, u32[]{:S(2)}, u32[]{:S(2)}) async-start(bf16[8,72,2048]{2,1,0:T(8,128)(2,1)} %bitcast.50), calls=%async_computation.2 | async-start | bytes 4718592 | tf_op jit(solution)/shard_map/all_to_all | solution.py:66
  95.0 59.1 %all-to-all-start.1 = ((bf16[8,72,2048]{2,1,0:T(8,128)(2,1)}), bf16[8,72,2048]{2,1,0:T(8,128)(2,1)}, u32[]{:S(2)}, u32[]{:S(2)}) async-start(bf16[8,72,2048]{2,1,0:T(8,128)(2,1)} %bitcast.49), calls=%async_computation.1 | async-start | bytes 4718592 | tf_op jit(solution)/shard_map/all_to_all | solution.py:67
  99.4 225.9 %reduce-scatter.8.cloned.1.call-start = ((), (), s32[]{:S(2)}) async-start(), calls=%async_computation.10 | async-start | bytes 7864320 | tf_op jit(solution)/shard_map/reduce_scatter | solution.py:107
  99.8 5.0 %copy-start.1 = (bf16[1,2048,768]{2,1,0:T(8,128)(2,1)S(1)}, bf16[1,2048,768]{2,1,0:T(8,128)(2,1)}, u32[]{:S(2)}) copy-start(bf16[1,2048,768]{2,1,0:T(8,128)(2,1)} %param.12) | copy-start | bytes 9437188
  162.4 165.4 %reduce-scatter.6.cloned.1.call-start = ((), (), s32[]{:S(2)}) async-start(), calls=%async_computation.9 | async-start | bytes 7864320 | tf_op jit(solution)/shard_map/reduce_scatter | solution.py:106
  169.6 0.9 copy-start.3
  176.8 201.3 %reduce-scatter.4.cloned.1.call-start = ((), (), s32[]{:S(2)}) async-start(), calls=%async_computation.8 | async-start | bytes 7864320 | tf_op jit(solution)/shard_map/reduce_scatter | solution.py:105
  184.9 11.1 %all-to-all-start.4 = ((f32[8,1,72]{2,1,0:T(1,128)}), f32[8,1,72]{2,1,0:T(1,128)S(1)}, u32[]{:S(2)}, u32[]{:S(2)}) async-start(f32[8,1,72]{2,1,0:T(1,128)} %all_to_all.26), calls=%async_computation.4 | async-start | bytes 8192 | tf_op jit(solution)/shard_map/all_to_all | solution.py:88
  188.3 3.5 copy-start.2
  188.3 3.5 copy-start.4
  196.1 110.3 %all-to-all-start.3 = ((f32[8,72,2048]{2,1,0:T(8,128)}), f32[8,72,2048]{2,1,0:T(8,128)}, u32[]{:S(2)}, u32[]{:S(2)}) async-start(f32[8,72,2048]{2,1,0:T(8,128)} %bitcast.51), calls=%async_computation.3 | async-start | bytes 9437184 | tf_op jit(solution)/shard_map/all_to_all | solution.py:81
Sparse Core Ops, SparseCore 0:
  162.5 69.1 reduce-scatter.7
  234.6 70.2 reduce-scatter.5
  307.9 70.2 reduce-scatter.3
where the time goes:
time: 388 us; the launch traced here: 387 us
  waiting for transfers between devices  238 us (61%)
  local copies, waits for them, and re-layouts  47.9 us (12%)
  matrix products  46.5 us (12%)
  starting transfers between devices  24.6 us (6%)
  other arithmetic  15.7 us (4%)
  between operations  13.9 us (4%)
    all_to_all x1, waiting for transfers between devices, per_device(): lax.all_to_all(row_grad.reshape(n_experts, capacity, model_width), 'exper...  101 us
    reduce_scatter x1, waiting for transfers between devices, per_device(): lax.psum_scatter(gate_term, 'dp', scatter_dimension=1, tiled=True)  48 us
    all_to_all x1, waiting for transfers between devices, per_device(): lax.all_to_all(send_x, 'expert', split_axis=0, concat_axis=0, tiled=True)  44.9 us
    all_to_all x1, waiting for transfers between devices, per_device(): lax.all_to_all(send_dy, 'expert', split_axis=0, concat_axis=0, tiled=True)  44.4 us
    dot_general x3, matrix products, outer_rows(): lax.dot_general(left, right, (((0,), (0,)), ((), ())), preferred_element_...  21.6 us
    gather x1, local copies, waits for them, and re-layouts, per_device(): send_dy = grad_pad[token_row].reshape(n_experts, capacity, model_width)  7.97 us
    gather x1, local copies, waits for them, and re-layouts, per_device(): send_x = tokens_pad[token_row].reshape(n_experts, capacity, model_width)  7.95 us
    gather x1, local copies, waits for them, and re-layouts, per_device(): picked_rows = back_rows.reshape(slot_rows, model_width)[position]  7.8 us
  transfers between devices with their start and end apart: 8, of which 4 were waited for; matrix products, arithmetic and copies ran while one was open for 22% of the time, Pallas kernels for 0%

commit v1 on v0

v1 whole, which is shorter than its diff:
```python
import jax
import jax.numpy as jnp
from jax import lax
from jax.sharding import PartitionSpec as P


def rows_dot(left, right):
    return lax.dot_general(
        left, right, (((1,), (1,)), ((), ())), preferred_element_type=jnp.float32
    )


def outer_rows(left, right):
    return lax.dot_general(
        left, right, (((0,), (0,)), ((), ())), preferred_element_type=jnp.float32
    )


def per_device(tokens, out_grad, gate_probs, expert_ids, w_gate, w_up, w_down):
    n_experts = lax.axis_size("expert")
    me = lax.axis_index("expert")
    tok_rows, model_width = tokens.shape
    top_k = expert_ids.shape[1]
    capacity = tok_rows * top_k * 9 // (8 * n_experts)
    slot_rows = n_experts * capacity
    group_rows = n_experts * tok_rows

    route = jnp.concatenate([expert_ids.astype(jnp.bfloat16), gate_probs], axis=1).T
    routes = lax.all_gather(route, "expert", axis=0, tiled=False)
    x_all = lax.all_gather(tokens, "expert", axis=0, tiled=True)
    dy_all = lax.all_gather(out_grad, "expert", axis=0, tiled=True)

    ids_all = routes[:, :top_k].astype(jnp.int32)
    probs_all = routes[:, top_k:].astype(jnp.float32)
    chosen = ids_all == me
    mine = jnp.any(chosen, axis=1).reshape(group_rows)
    prob_tok = jnp.sum(jnp.where(chosen, probs_all, 0.0), axis=1).reshape(group_rows)
    rank = jnp.cumsum(mine.astype(jnp.int32)) - 1
    slot_of = jnp.where(mine, rank, -1)
    hit = slot_of[None, :] == jnp.arange(slot_rows, dtype=jnp.int32)[:, None]
    pick = hit.astype(jnp.bfloat16)
    prob_slots = jnp.sum(jnp.where(hit, prob_tok[None, :], 0.0), axis=1, keepdims=True)

    gate_mat, up_mat, down_mat = w_gate[0], w_up[0], w_down[0]
    x_slots = jnp.dot(pick, x_all, preferred_element_type=jnp.float32).astype(jnp.bfloat16)
    gate_pre = jnp.dot(x_slots, gate_mat, preferred_element_type=jnp.float32)
    up_pre = jnp.dot(x_slots, up_mat, preferred_element_type=jnp.float32)
    sig = jax.nn.sigmoid(gate_pre)
    silu = gate_pre * sig
    hidden_act = silu * up_pre
    hidden = hidden_act.astype(jnp.bfloat16)

    dy_slots = jnp.dot(pick, dy_all, preferred_element_type=jnp.float32).astype(jnp.bfloat16)
    grad_hidden = rows_dot(dy_slots, down_mat)
    prob_grad = jnp.sum(hidden_act * grad_hidden, axis=1, keepdims=True)
    scaled_hidden = prob_slots * grad_hidden
    grad_gate = (scaled_hidden * up_pre * sig * (1.0 + gate_pre * (1.0 - sig))).astype(
        jnp.bfloat16
    )
    grad_up = (scaled_hidden * silu).astype(jnp.bfloat16)
    scaled_dy = (prob_slots * dy_slots.astype(jnp.float32)).astype(jnp.bfloat16)

    down_term = outer_rows(hidden, scaled_dy).astype(jnp.bfloat16)
    down_sum = lax.psum_scatter(down_term, "dp", scatter_dimension=0, tiled=True)
    gate_term = outer_rows(grad_gate, x_slots).astype(jnp.bfloat16)
    gate_sum = lax.psum_scatter(gate_term, "dp", scatter_dimension=0, tiled=True)
    up_term = outer_rows(grad_up, x_slots).astype(jnp.bfloat16)
    up_sum = lax.psum_scatter(up_term, "dp", scatter_dimension=0, tiled=True)

    row_grad = rows_dot(
        jnp.concatenate([grad_gate, grad_up], axis=1),
        jnp.concatenate([gate_mat, up_mat], axis=1),
    ).astype(jnp.bfloat16)
    part = outer_rows(pick, row_grad).astype(jnp.bfloat16)
    tokens_grad = lax.psum_scatter(part, "expert", scatter_dimension=0, tiled=True)

    prob_back = jnp.sum(jnp.where(hit, prob_grad, 0.0), axis=0)
    prob_back = prob_back.reshape(n_experts, 1, tok_rows)
    prob_part = jnp.where(chosen, prob_back, 0.0)
    probs_grad = lax.psum_scatter(prob_part, "expert", scatter_dimension=0, tiled=False).T
    return (tokens_grad, probs_grad, gate_sum.T[None], up_sum.T[None], down_sum[None])


def solution(mesh):
    in_specs = (
        P(("dp", "expert"), None),
        P(("dp", "expert"), None),
        P(("dp", "expert"), None),
        P(("dp", "expert"), None),
        P("expert", None, None),
        P("expert", None, None),
        P("expert", None, None),
    )
    out_specs = (
        P(("dp", "expert"), None),
        P(("dp", "expert"), None),
        P("expert", None, "dp"),
        P("expert", None, "dp"),
        P("expert", "dp", None),
    )
    return jax.shard_map(
        per_device, mesh=mesh, in_specs=in_specs, out_specs=out_specs, check_vma=False
    )
```

time: 388 us -> 318 us (0.82)
  local copies, waits for them, and re-layouts: 47.9 us -> 3.53 us
  blocking collectives: 0 us -> 41.1 us
  waiting for transfers between devices: 238 us -> 204 us
  starting transfers between devices: 24.6 us -> 0.42 us
  other arithmetic: 15.7 us -> 6.94 us
    all_to_all x5 -> x0, waiting for transfers between devices: 190 us -> none  [the longest x1 101 us: per_device(): lax.all_to_all(row_grad.reshape(n_experts, capacity, model_width), 'exper...]
    reduce_scatter x2 -> x3, waiting for transfers between devices: 48 us -> 132 us  [the longest x1 52.7 us: per_device(): lax.psum_scatter(part, 'expert', scatter_dimension=0, tiled=True)]
    all_gather x0 -> x2, waiting for transfers between devices: none -> 70.2 us  [the longest x1 35.8 us: per_device(): dy_all = lax.all_gather(out_grad, 'expert', axis=0, tiled=True)]
    gather x5 -> x0, local copies, waits for them, and re-layouts: 29.9 us -> none  [the longest x1 7.97 us: per_device(): send_dy = grad_pad[token_row].reshape(n_experts, capacity, model_width)]
    unnamed x0 -> x1, blocking collectives: none -> 26.7 us
    all_to_all x5 -> x0, starting transfers between devices: 24 us -> none  [the longest x1 6.33 us: per_device(): lax.all_to_all(send_prob, 'expert', split_axis=0, concat_axis=0, tiled=True)]
    all_gather x0 -> x1, blocking collectives: none -> 14.4 us  [per_device(): routes = lax.all_gather(route, 'expert', axis=0, tiled=False)]
    broadcast_in_dim x3 -> x0, other arithmetic: 7.19 us -> none  [the longest x1 2.4 us: per_device(): down_weight_grad = down_sum.astype(jnp.bfloat16)[None]]
  transfers between devices with their start and end apart: 8 -> 6, of which waited for: 4 -> 5; matrix products, arithmetic and copies ran while one was open for 22% -> 14% of each run, Pallas kernels for 0% -> 0%
where the time goes in v1:
time: 318 us
  waiting for transfers between devices  204 us (64%)
  matrix products  47.9 us (15%)
  blocking collectives  41.1 us (13%)
  between operations  14.2 us (4%)
  other arithmetic  6.94 us (2%)
  local copies, waits for them, and re-layouts  3.53 us (1%)
    reduce_scatter x1, waiting for transfers between devices, per_device(): lax.psum_scatter(part, 'expert', scatter_dimension=0, tiled=True)  52.7 us
    reduce_scatter x1, waiting for transfers between devices, per_device(): up_sum = lax.psum_scatter(up_term, 'dp', scatter_dimension=0, tiled=True)  47.4 us
    all_gather x1, waiting for transfers between devices, per_device(): dy_all = lax.all_gather(out_grad, 'expert', axis=0, tiled=True)  35.8 us
    all_gather x1, waiting for transfers between devices, per_device(): x_all = lax.all_gather(tokens, 'expert', axis=0, tiled=True)  34.4 us
    reduce_scatter x1, waiting for transfers between devices, per_device(): lax.psum_scatter(gate_term, 'dp', scatter_dimension=0, tiled=True)  32.1 us
    unnamed x1, blocking collectives  26.7 us
    dot_general x4, matrix products, outer_rows(): lax.dot_general(left, right, (((0,), (0,)), ((), ())), preferred_element_...  20.1 us
    all_gather x1, blocking collectives, per_device(): routes = lax.all_gather(route, 'expert', axis=0, tiled=False)  14.4 us
  transfers between devices with their start and end apart: 6, of which 5 were waited for; matrix products, arithmetic and copies ran while one was open for 14% of the time, Pallas kernels for 0%

profile of v1, /device:TPU:0, one launch (start us, length us, event | category | flops | bytes accessed | tf_op | source)
XLA Modules:
  0.0 317.9 jit_solution(273025088158786395)
XLA Ops:
  7.2 0.7 all-gather.6.cloned.1.call-update
  8.0 0.7 all-gather.4.cloned.1.call-update
  8.7 0.7 convert_element_type.50
  9.4 0.7 maximum_bitcast_fusion
  10.1 14.4 %all-gather = bf16[64,128]{1,0:T(8,128)(2,1)S(1)} all-gather(bf16[8,128]{1,0:T(8,128)(2,1)S(1)} %maximum_bitcast_fusion), channel_id=2, replica_groups=mesh['dp'=4,'expert'=8] {'expert'}, dimensions={0}, use_global_device_ids=true | all-gather | bytes 18432 | tf_op jit(solution)/shard_map/all_gather | solution.py:29
  24.5 0.3 reduce-window.9
  24.8 0.1 slice.14
  24.9 0.1 slice_reduce_fusion
  25.0 0.1 select_bitcast_fusion
  25.1 34.4 %all-gather.6.cloned.1.call-done = bf16[1024,2048]{1,0:T(8,128)(2,1)} async-done(((bf16[128,2048]{1,0:T(8,128)(2,1)}), bf16[1024,2048]{1,0:T(8,128)(2,1)}) %all-gather.6.cloned.1.call-update) | async-done | bytes 4194320 | tf_op jit(solution)/shard_map/all_gather | solution.py:30
  59.5 5.1 %convolution_convert_fusion.4 = bf16[576,2048]{1,0:T(8,128)(2,1)S(1)} fusion(bf16[1024,2048]{1,0:T(8,128)(2,1)} %all-gather.6.cloned.1.call-done, s32[1024]{0:T(1024)S(1)} %select_bitcast_fusion), kind=kOutput, calls=%fused_computation.12 | convolution fusion | flops 2417688576 | bytes 6557696 | tf_op jit(solution)/shard_map/dot_general | solution.py:45
  64.7 3.3 %fusion.20 = f32[576,768]{1,0:T(8,128)} fusion(bf16[576,2048]{1,0:T(8,128)(2,1)S(1)} %convolution_convert_fusion.4, bf16[1,2048,768]{2,1,0:T(8,128)(2,1)S(1)} %copy-done.5), kind=kOutput, calls=%fused_computation.39 | convolution fusion | flops 1811939328 | bytes 7274496 | tf_op jit(solution)/shard_map/dot_general | solution.py:46
  68.0 3.3 %fusion.22 = f32[576,768]{1,0:T(8,128)} fusion(bf16[576,2048]{1,0:T(8,128)(2,1)S(1)} %convolution_convert_fusion.4, bf16[1,2048,768]{2,1,0:T(8,128)(2,1)S(1)} %copy-done.4), kind=kOutput, calls=%fused_computation.41 | convolution fusion | flops 1811939328 | bytes 7274496 | tf_op jit(solution)/shard_map/dot_general | solution.py:47
  71.3 35.8 %all-gather.4.cloned.1.call-done = bf16[1024,2048]{1,0:T(8,128)(2,1)} async-done(((bf16[128,2048]{1,0:T(8,128)(2,1)}), bf16[1024,2048]{1,0:T(8,128)(2,1)}) %all-gather.4.cloned.1.call-update) | async-done | bytes 4194320 | tf_op jit(solution)/shard_map/all_gather | solution.py:31
  107.1 5.1 %convolution_convert_fusion.5 = bf16[576,2048]{1,0:T(8,128)(2,1)S(1)} fusion(bf16[1024,2048]{1,0:T(8,128)(2,1)} %all-gather.4.cloned.1.call-done, s32[1024]{0:T(1024)S(1)} %select_bitcast_fusion), kind=kOutput, calls=%fused_computation.13 | convolution fusion | flops 2417688576 | bytes 6557696 | tf_op jit(solution)/shard_map/dot_general | solution.py:53
  112.2 3.4 %multiply_reduce_fusion = (f32[576]{0:T(1024)S(1)}, f32[576,768]{1,0:T(8,128)}) fusion(f32[576,768]{1,0:T(8,128)S(1)} %copy-done.2, f32[576,768]{1,0:T(8,128)S(1)} %copy-done.1, bf16[576,2048]{1,0:T(8,128)(2,1)S(1)} %convolution_convert_fusion.5, bf16[1,768,2048]{2,1,0:T(8,128)(2,1)S(1)} %copy-done), kind=kOutput, calls=%fused_computation.21 | convolution fusion | flops 1815035392 | bytes 10815744 | tf_op jit(solution)/shard_map/dot_general | solution.py:8
  115.6 0.6 select_reduce_fusion
  116.2 4.4 %convolution_convert_fusion.1 = bf16[768,2048]{1,0:T(8,128)(2,1)} fusion(bf16[576,2048]{1,0:T(8,128)(2,1)S(1)} %convolution_convert_fusion.5, f32[576]{0:T(1024)S(1)} %get-tuple-element.6, f32[576,768]{1,0:T(8,128)S(1)} %copy-done.2, f32[576,768]{1,0:T(8,128)S(1)} %copy-done.1), kind=kOutput, calls=%fused_computation.6 | convolution fusion | flops 1819705344 | bytes 9046272 | tf_op jit(solution)/shard_map/dot_general | solution.py:14
  120.7 0.2 reduce-scatter.7.cloned.1.call-start
  120.9 4.5 %multiply_convert_fusion.3 = (bf16[576,768]{1,0:T(8,128)(2,1)S(1)}, bf16[576,768]{1,0:T(8,128)(2,1)}) fusion(f32[576,768]{1,0:T(8,128)} %fusion.20, f32[576,768]{1,0:T(8,128)} %fusion.22, f32[576,768]{1,0:T(8,128)} %get-tuple-element.12, f32[576]{0:T(1024)S(1)} %get-tuple-element.6), kind=kLoop, calls=%fused_computation.23 | loop fusion | flops 6193152 | bytes 7080192 | tf_op jit(solution)/shard_map/convert_element_type | solution.py:57
  125.4 0.9 copy-done.3
  126.4 4.1 %convolution_convert_fusion.3 = bf16[768,2048]{1,0:T(8,128)(2,1)} fusion(bf16[576,768]{1,0:T(8,128)(2,1)S(1)} %get-tuple-element.9, bf16[576,2048]{1,0:T(8,128)(2,1)S(1)} %copy-done.8), kind=kOutput, calls=%fused_computation.8 | convolution fusion | flops 1813512192 | bytes 6389760 | tf_op jit(solution)/shard_map/dot_general | solution.py:14
  130.5 6.5 %convolution_convert_fusion.2 = bf16[768,2048]{1,0:T(8,128)(2,1)} fusion(bf16[576,768]{1,0:T(8,128)(2,1)} %get-tuple-element.10, bf16[576,2048]{1,0:T(8,128)(2,1)} %copy-done.7), kind=kOutput, calls=%fused_computation.7 | convolution fusion | flops 1813512192 | bytes 6389760 | tf_op jit(solution)/shard_map/dot_general | solution.py:14
  137.1 7.5 %fusion.6 = bf16[576,2048]{1,0:T(8,128)(2,1)S(1)} fusion(bf16[2048,768]{1,0:T(8,128)(2,1)} %bitcast.43, bf16[2048,768]{1,0:T(8,128)(2,1)} %bitcast.44, bf16[576,768]{1,0:T(8,128)(2,1)} %get-tuple-element.10, bf16[576,768]{1,0:T(8,128)(2,1)} %copy-done.3), kind=kOutput, calls=%fused_computation.11 | convolution fusion | flops 3641180160 | bytes 10420224 | tf_op jit(solution)/shard_map/dot_general | solution.py:8
  144.6 5.1 %convolution_convert_fusion = bf16[1024,2048]{1,0:T(8,128)(2,1)} fusion(bf16[576,2048]{1,0:T(8,128)(2,1)S(1)} %fusion.6, s32[1024]{0:T(1024)S(1)} %select_bitcast_fusion), kind=kOutput, calls=%fused_computation.5 | convolution fusion | flops 2418606080 | bytes 6557696 | tf_op jit(solution)/shard_map/dot_general | solution.py:14
  149.8 0.6 copy-done.6
  150.4 0.6 dynamic-slice
  151.0 26.7 %all-reduce = f32[8,4,128]{2,1,0:T(4,128)S(1)} all-reduce(f32[8,4,128]{2,1,0:T(4,128)S(1)} %broadcast_select_fusion), channel_id=4, replica_groups=mesh['dp'=4,'expert'=8] {'expert'}, use_global_device_ids=true, to_apply=%region_8.9.clone | all-reduce | flops 4096 | bytes 32768
  177.7 1.1 dynamic-slice_bitcast_fusion
  178.8 32.1 %reduce-scatter.7.cloned.1.call-done = bf16[192,2048]{1,0:T(8,128)(2,1)} async-done(((bf16[768,2048]{1,0:T(8,128)(2,1)}), bf16[192,2048]{1,0:T(8,128)(2,1)}) %reduce-scatter.7.cloned.1.call-update) | async-done | bytes 786448 | tf_op jit(solution)/shard_map/reduce_scatter | solution.py:66
  210.9 47.4 %reduce-scatter.9.cloned.1.call-done = bf16[192,2048]{1,0:T(8,128)(2,1)} async-done(((bf16[768,2048]{1,0:T(8,128)(2,1)}), bf16[192,2048]{1,0:T(8,128)(2,1)}) %reduce-scatter.9.cloned.1.call-update) | async-done | bytes 786448 | tf_op jit(solution)/shard_map/reduce_scatter | solution.py:68
  258.3 52.7 %reduce-scatter.5.cloned.1.call-done = bf16[128,2048]{1,0:T(8,128)(2,1)} async-done(((bf16[1024,2048]{1,0:T(8,128)(2,1)}), bf16[128,2048]{1,0:T(8,128)(2,1)}) %reduce-scatter.5.cloned.1.call-update) | async-done | bytes 524304 | tf_op jit(solution)/shard_map/reduce_scatter | solution.py:75
  (31 shorter events, 0.4 us)
Async XLA Ops:
  7.2 105.0 %copy-start = (bf16[1,768,2048]{2,1,0:T(8,128)(2,1)S(1)}, bf16[1,768,2048]{2,1,0:T(8,128)(2,1)}, u32[]{:S(2)}) copy-start(bf16[1,768,2048]{2,1,0:T(8,128)(2,1)} %param.13) | copy-start | bytes 9437188
  7.2 52.3 %all-gather.6.cloned.1.call-start = ((), (), s32[]{:S(2)}) async-start(), calls=%async_computation.5 | async-start | bytes 4718592 | tf_op jit(solution)/shard_map/all_gather | solution.py:30
  7.9 99.1 %all-gather.4.cloned.1.call-start = ((), (), s32[]{:S(2)}) async-start(), calls=%async_computation.4 | async-start | bytes 4718592 | tf_op jit(solution)/shard_map/all_gather | solution.py:31
  8.7 170.2 %reduce-scatter.11.cloned.1.call-start = ((), (), s32[]{:S(2)}) async-start(), calls=%async_computation.9 | async-start | bytes 3932160 | tf_op jit(solution)/shard_map/reduce_scatter | solution.py:64
  59.5 5.2 %copy-start.5 = (bf16[1,2048,768]{2,1,0:T(8,128)(2,1)S(1)}, bf16[1,2048,768]{2,1,0:T(8,128)(2,1)}, u32[]{:S(2)}) copy-start(bf16[1,2048,768]{2,1,0:T(8,128)(2,1)} %param.11) | copy-start | bytes 9437188
  64.7 3.3 %copy-start.7 = (bf16[576,2048]{1,0:T(8,128)(2,1)}, bf16[576,2048]{1,0:T(8,128)(2,1)S(1)}, u32[]{:S(2)}) copy-start(bf16[576,2048]{1,0:T(8,128)(2,1)S(1)} %convolution_convert_fusion.4) | copy-start | bytes 7077892
  64.7 3.3 %copy-start.4 = (bf16[1,2048,768]{2,1,0:T(8,128)(2,1)S(1)}, bf16[1,2048,768]{2,1,0:T(8,128)(2,1)}, u32[]{:S(2)}) copy-start(bf16[1,2048,768]{2,1,0:T(8,128)(2,1)} %param.12) | copy-start | bytes 9437188
  107.0 5.2 %copy-start.1 = (f32[576,768]{1,0:T(8,128)S(1)}, f32[576,768]{1,0:T(8,128)}, u32[]{:S(2)}) copy-start(f32[576,768]{1,0:T(8,128)} %fusion.20) | copy-start | bytes 5308420
  107.0 5.2 %copy-start.2 = (f32[576,768]{1,0:T(8,128)S(1)}, f32[576,768]{1,0:T(8,128)}, u32[]{:S(2)}) copy-start(f32[576,768]{1,0:T(8,128)} %fusion.22) | copy-start | bytes 5308420
  120.7 90.2 %reduce-scatter.7.cloned.1.call-start = ((), (), s32[]{:S(2)}) async-start(), calls=%async_computation.7 | async-start | bytes 3932160 | tf_op jit(solution)/shard_map/reduce_scatter | solution.py:66
  120.9 5.4 %copy-start.8 = (bf16[576,2048]{1,0:T(8,128)(2,1)S(1)}, bf16[576,2048]{1,0:T(8,128)(2,1)}, u32[]{:S(2)}) copy-start(bf16[576,2048]{1,0:T(8,128)(2,1)} %copy-done.7) | copy-start | bytes 7077892
  125.4 0.9 copy-start.3
  130.5 127.8 %reduce-scatter.9.cloned.1.call-start = ((), (), s32[]{:S(2)}) async-start(), calls=%async_computation.8 | async-start | bytes 3932160 | tf_op jit(solution)/shard_map/reduce_scatter | solution.py:68
  137.1 174.0 %reduce-scatter.5.cloned.1.call-start = ((), (), s32[]{:S(2)}) async-start(), calls=%async_computation.6 | async-start | bytes 4718592 | tf_op jit(solution)/shard_map/reduce_scatter | solution.py:75
  149.7 0.7 copy-start.6
Sparse Core Ops, SparseCore 0:
  9.6 49.8 all-gather.5
  61.1 45.9 all-gather.3
  120.8 42.6 reduce-scatter.10
  167.0 43.9 reduce-scatter.6
  214.3 43.9 reduce-scatter.8
  261.0 49.9 reduce-scatter.4

commit v2 on v1

--- a/solution.py
+++ b/solution.py
@@ -14,6 +14,27 @@
     return lax.dot_general(
         left, right, (((0,), (0,)), ((), ())), preferred_element_type=jnp.float32
     )
+
+
+def halve(blocks, bit, axis):
+    n_dp = lax.axis_size("dp")
+    mine = (lax.axis_index("dp") // bit) % 2
+    keep = lax.dynamic_index_in_dim(blocks, mine, axis, keepdims=False)
+    give = lax.dynamic_index_in_dim(blocks, 1 - mine, axis, keepdims=False)
+    got = lax.ppermute(give, "dp", [(d, d ^ bit) for d in range(n_dp)])
+    return (keep.astype(jnp.float32) + got.astype(jnp.float32)).astype(jnp.bfloat16)
+
+
+def dp_sum(term):
+    n_dp = lax.axis_size("dp")
+    if n_dp != 4:
+        return lax.psum_scatter(term, "dp", scatter_dimension=0, tiled=True)
+    rows, columns = term.shape
+    blocks = term.reshape(2, 2, rows // 4, columns)
+    left, right = blocks[..., : columns // 2], blocks[..., columns // 2 :]
+    left = halve(halve(left, 1, 1), 2, 0)
+    right = halve(halve(right, 2, 0), 1, 0)
+    return jnp.concatenate([left, right], axis=1)
 
 
 def per_device(tokens, out_grad, gate_probs, expert_ids, w_gate, w_up, w_down):
@@ -60,24 +81,31 @@
     grad_up = (scaled_hidden * silu).astype(jnp.bfloat16)
     scaled_dy = (prob_slots * dy_slots.astype(jnp.float32)).astype(jnp.bfloat16)
 
-    down_term = outer_rows(hidden, scaled_dy).astype(jnp.bfloat16)
-    down_sum = lax.psum_scatter(down_term, "dp", scatter_dimension=0, tiled=True)
-    gate_term = outer_rows(grad_gate, x_slots).astype(jnp.bfloat16)
-    gate_sum = lax.psum_scatter(gate_term, "dp", scatter_dimension=0, tiled=True)
-    up_term = outer_rows(grad_up, x_slots).astype(jnp.bfloat16)
-    up_sum = lax.psum_scatter(up_term, "dp", scatter_dimension=0, tiled=True)
+    down_sum = dp_sum(outer_rows(hidden, scaled_dy).astype(jnp.bfloat16))
 
     row_grad = rows_dot(
         jnp.concatenate([grad_gate, grad_up], axis=1),
         jnp.concatenate([gate_mat, up_mat], axis=1),
     ).astype(jnp.bfloat16)
-    part = outer_rows(pick, row_grad).astype(jnp.bfloat16)
-    tokens_grad = lax.psum_scatter(part, "expert", scatter_dimension=0, tiled=True)
+    prob_high = lax.reduce_precision(prob_grad, 8, 7)
+    prob_low = prob_grad - prob_high
+    extra = -(-2 * n_experts // 128) * 128
+    column = jnp.arange(extra, dtype=jnp.int32)[None, :]
+    prob_columns = jnp.where(column == me, prob_high, 0.0) + jnp.where(
+        column == me + n_experts, prob_low, 0.0
+    )
+    back = jnp.concatenate([row_grad, prob_columns.astype(jnp.bfloat16)], axis=1)
+    part = outer_rows(pick, back).astype(jnp.bfloat16)
+    total = lax.psum_scatter(part, "expert", scatter_dimension=0, tiled=True)
+    tokens_grad = total[:, :model_width]
+    prob_terms = total[:, model_width : model_width + 2 * n_experts].astype(jnp.float32)
+    prob_experts = prob_terms[:, :n_experts] + prob_terms[:, n_experts:]
+    own = expert_ids[:, :, None] == jnp.arange(n_experts, dtype=jnp.int32)[None, None, :]
+    probs_grad = jnp.sum(jnp.where(own, prob_experts[:, None, :], 0.0), axis=2)
 
-    prob_back = jnp.sum(jnp.where(hit, prob_grad, 0.0), axis=0)
-    prob_back = prob_back.reshape(n_experts, 1, tok_rows)
-    prob_part = jnp.where(chosen, prob_back, 0.0)
-    probs_grad = lax.psum_scatter(prob_part, "expert", scatter_dimension=0, tiled=False).T
+    x_late, _ = lax.optimization_barrier((x_slots, part))
+    gate_sum = dp_sum(outer_rows(grad_gate, x_late).astype(jnp.bfloat16))
+    up_sum = dp_sum(outer_rows(grad_up, x_late).astype(jnp.bfloat16))
     return (tokens_grad, probs_grad, gate_sum.T[None], up_sum.T[None], down_sum[None])
 
 

time: 318 us -> 227 us (0.71)
  waiting for transfers between devices: 204 us -> 126 us
  blocking collectives: 41.1 us -> 14.4 us
  starting transfers between devices: 0.42 us -> 15.2 us
  matrix products: 47.9 us -> 40.3 us
  local copies, waits for them, and re-layouts: 3.53 us -> 7.91 us
    reduce_scatter x4 -> x1, waiting for transfers between devices: 132 us -> 0.01 us  [per_device(): total = lax.psum_scatter(part, 'expert', scatter_dimension=0, tiled=True)]
    ppermute x0 -> x12, waiting for transfers between devices: none -> 52.5 us  [halve(): got = lax.ppermute(give, 'dp', [(d, d ^ bit) for d in range(n_dp)])]
    unnamed x1 -> x0, blocking collectives: 26.7 us -> none
    ppermute x0 -> x12, starting transfers between devices: none -> 15.1 us  [halve(): got = lax.ppermute(give, 'dp', [(d, d ^ bit) for d in range(n_dp)])]
    dot_general x2, matrix products: 10.9 us -> 5.88 us  [rows_dot(): lax.dot_general(left, right, (((1,), (1,)), ((), ())), preferred_element_...]
  transfers between devices with their start and end apart: 6 -> 15, of which waited for: 5 -> 8; matrix products, arithmetic and copies ran while one was open for 14% -> 13% of each run, Pallas kernels for 0% -> 0%
where the time goes in v2:
time: 227 us
  waiting for transfers between devices  126 us (56%)
  matrix products  40.3 us (18%)
  starting transfers between devices  15.2 us (7%)
  blocking collectives  14.4 us (6%)
  between operations  14.3 us (6%)
  other arithmetic  9.29 us (4%)
  local copies, waits for them, and re-layouts  7.91 us (3%)
    ppermute x12, waiting for transfers between devices, halve(): got = lax.ppermute(give, 'dp', [(d, d ^ bit) for d in range(n_dp)])  52.5 us
    all_gather x1, waiting for transfers between devices, per_device(): dy_all = lax.all_gather(out_grad, 'expert', axis=0, tiled=True)  37.7 us
    all_gather x1, waiting for transfers between devices, per_device(): x_all = lax.all_gather(tokens, 'expert', axis=0, tiled=True)  34.1 us
    dot_general x4, matrix products, outer_rows(): lax.dot_general(left, right, (((0,), (0,)), ((), ())), preferred_element_...  17.3 us
    ppermute x12, starting transfers between devices, halve(): got = lax.ppermute(give, 'dp', [(d, d ^ bit) for d in range(n_dp)])  15.1 us
    all_gather x1, blocking collectives, per_device(): routes = lax.all_gather(route, 'expert', axis=0, tiled=False)  14.4 us
    dot_general x2, matrix products, rows_dot(): lax.dot_general(left, right, (((1,), (1,)), ((), ())), preferred_element_...  5.88 us
    dot_general x1, matrix products, per_device(): jnp.dot(pick, x_all, preferred_element_type=jnp.float32)  5.14 us
  transfers between devices with their start and end apart: 15, of which 8 were waited for; matrix products, arithmetic and copies ran while one was open for 13% of the time, Pallas kernels for 0%

profile of v2, /device:TPU:0, one launch (start us, length us, event | category | flops | bytes accessed | tf_op | source)
XLA Modules:
  0.0 227.1 jit_solution(15863169879821645315)
XLA Ops:
  10.1 14.4 %all-gather = bf16[64,128]{1,0:T(8,128)(2,1)S(1)} all-gather(bf16[8,128]{1,0:T(8,128)(2,1)S(1)} %maximum_bitcast_fusion.3), channel_id=2, replica_groups=mesh['dp'=4,'expert'=8] {'expert'}, dimensions={0}, use_global_device_ids=true | all-gather | bytes 18432 | tf_op jit(solution)/shard_map/all_gather | solution.py:50
  25.4 34.1 %all-gather.6.cloned.1.call-done = bf16[1024,2048]{1,0:T(8,128)(2,1)} async-done(((bf16[128,2048]{1,0:T(8,128)(2,1)}), bf16[1024,2048]{1,0:T(8,128)(2,1)}) %all-gather.6.cloned.1.call-update) | async-done | bytes 4194320 | tf_op jit(solution)/shard_map/all_gather | solution.py:51
  59.5 5.1 %convolution_convert_fusion.4 = bf16[576,2048]{1,0:T(8,128)(2,1)S(1)} fusion(bf16[1024,2048]{1,0:T(8,128)(2,1)} %all-gather.6.cloned.1.call-done, s32[1024]{0:T(1024)S(1)} %select_bitcast_fusion), kind=kOutput, calls=%fused_computation.12 | convolution fusion | flops 2417688576 | bytes 6557696 | tf_op jit(solution)/shard_map/dot_general | solution.py:66
  64.7 1.4 copy-done.6
  66.1 3.2 %fusion.38 = f32[576,768]{1,0:T(8,128)} fusion(bf16[576,2048]{1,0:T(8,128)(2,1)S(1)} %convolution_convert_fusion.4, bf16[1,2048,768]{2,1,0:T(8,128)(2,1)S(1)} %copy-done.3), kind=kOutput, calls=%fused_computation.89 | convolution fusion | flops 1811939328 | bytes 7274496 | tf_op jit(solution)/shard_map/dot_general | solution.py:68
  69.3 37.7 %all-gather.4.cloned.1.call-done = bf16[1024,2048]{1,0:T(8,128)(2,1)} async-done(((bf16[128,2048]{1,0:T(8,128)(2,1)}), bf16[1024,2048]{1,0:T(8,128)(2,1)}) %all-gather.4.cloned.1.call-update) | async-done | bytes 4194320 | tf_op jit(solution)/shard_map/all_gather | solution.py:52
  107.0 5.0 %convolution_convert_fusion.5 = bf16[576,2048]{1,0:T(8,128)(2,1)S(1)} fusion(bf16[1024,2048]{1,0:T(8,128)(2,1)} %all-gather.4.cloned.1.call-done, s32[1024]{0:T(1024)S(1)} %select_bitcast_fusion), kind=kOutput, calls=%fused_computation.13 | convolution fusion | flops 2417688576 | bytes 6557696 | tf_op jit(solution)/shard_map/dot_general | solution.py:74
  112.1 2.0 fusion.4
  116.0 3.8 %multiply_convert_fusion.3 = (bf16[576,768]{1,0:T(8,128)(2,1)S(1)}, f32[576]{0:T(1024)S(1)}, bf16[576,768]{1,0:T(8,128)(2,1)S(1)}, f32[576,768]{1,0:T(8,128)}) fusion(f32[576,768]{1,0:T(8,128)S(1)} %copy-done.9, f32[576,768]{1,0:T(8,128)S(1)} %fusion.4, f32[576]{0:T(1024)S(1)} %select_reduce_fusion, bf16[576,2048]{1,0:T(8,128)(2,1)S(1)} %copy-done.7, ...), kind=kOutput, calls=%fused_computation.25 | convolution fusion | flops 1819459072 | bytes 12587520 | tf_op jit(solution)/shard_map/dot_general | solution.py:67
  120.1 3.8 %fusion.6 = bf16[576,2048]{1,0:T(8,128)(2,1)S(1)} fusion(bf16[2048,768]{1,0:T(8,128)(2,1)S(1)} %bitcast.105, bf16[2048,768]{1,0:T(8,128)(2,1)S(1)} %bitcast.106, bf16[576,768]{1,0:T(8,128)(2,1)S(1)} %get-tuple-element.9, bf16[576,768]{1,0:T(8,128)(2,1)S(1)} %get-tuple-element.7), kind=kOutput, calls=%fused_computation.11 | convolution fusion | flops 3641180160 | bytes 10420224 | tf_op jit(solution)/shard_map/dot_general | solution.py:8
  124.0 5.8 %convolution_convert_fusion = bf16[1024,2176]{1,0:T(8,128)(2,1)} fusion(bf16[576,128]{1,0:T(8,128)(2,1)S(1)} %add_convert_fusion, bf16[576,2048]{1,0:T(8,128)(2,1)S(1)} %fusion.6, s32[1024]{0:T(1024)S(1)} %select_bitcast_fusion), kind=kOutput, calls=%fused_computation.4 | convolution fusion | flops 2574745600 | bytes 6967296 | tf_op jit(solution)/shard_map/dot_general | solution.py:14
  129.8 5.6 %convolution_convert_fusion.1 = bf16[768,2048]{1,0:T(8,128)(2,1)S(1)} fusion(bf16[576,2048]{1,0:T(8,128)(2,1)} %copy-done.10, f32[576]{0:T(1024)S(1)} %select_reduce_fusion, f32[576,768]{1,0:T(8,128)} %fusion.38, f32[576,768]{1,0:T(8,128)} %get-tuple-element.18), kind=kOutput, calls=%fused_computation.6 | convolution fusion | flops 1819705344 | bytes 9046272 | tf_op jit(solution)/shard_map/dot_general | solution.py:14
  135.9 1.6 collective-permute-start.10
  137.5 1.5 collective-permute-start.8
  139.0 2.9 %convolution_convert_fusion.2 = bf16[768,2048]{1,0:T(8,128)(2,1)S(1)} fusion(bf16[576,768]{1,0:T(8,128)(2,1)S(1)} %copy-done.14, bf16[576,2048]{1,0:T(8,128)(2,1)S(1)} %copy-done.8), kind=kOutput, calls=%fused_computation.7 | convolution fusion | flops 1813512192 | bytes 6389760 | tf_op jit(solution)/shard_map/dot_general | solution.py:14
  143.1 3.1 %convolution_convert_fusion.3 = bf16[768,2048]{1,0:T(8,128)(2,1)S(1)} fusion(bf16[576,768]{1,0:T(8,128)(2,1)S(1)} %copy-done.12, bf16[576,2048]{1,0:T(8,128)(2,1)S(1)} %copy-done.8), kind=kOutput, calls=%fused_computation.8 | convolution fusion | flops 1813512192 | bytes 6389760 | tf_op jit(solution)/shard_map/dot_general | solution.py:14
  147.4 1.0 collective-permute-start.4
  148.3 1.1 collective-permute-start.2
  149.5 6.8 %collective-permute-done.10 = bf16[2,192,1024]{2,1,0:T(8,128)(2,1)S(1)} collective-permute-done((bf16[2,192,1024]{2,1,0:T(8,128)(2,1)S(1)}, bf16[2,192,1024]{2,1,0:T(8,128)(2,1)S(1)}, u32[]{:S(2)}, u32[]{:S(2)}) %collective-permute-start.10) | collective-permute-done | bytes 786464 | tf_op jit(solution)/shard_map/ppermute | solution.py:24
  156.3 1.5 collective-permute-start
  158.1 1.3 collective-permute-start.11
  159.8 13.4 %collective-permute-done.6 = bf16[2,192,1024]{2,1,0:T(8,128)(2,1)S(1)} collective-permute-done((bf16[2,192,1024]{2,1,0:T(8,128)(2,1)S(1)}, bf16[2,192,1024]{2,1,0:T(8,128)(2,1)S(1)}, u32[]{:S(2)}, u32[]{:S(2)}) %collective-permute-start.6) | collective-permute-done | bytes 786464 | tf_op jit(solution)/shard_map/ppermute | solution.py:24
  173.2 1.5 collective-permute-start.9
  175.0 1.5 collective-permute-start.7
  176.9 13.1 %collective-permute-done.2 = bf16[2,192,1024]{2,1,0:T(8,128)(2,1)S(1)} collective-permute-done((bf16[2,192,1024]{2,1,0:T(8,128)(2,1)S(1)}, bf16[2,192,1024]{2,1,0:T(8,128)(2,1)S(1)}, u32[]{:S(2)}, u32[]{:S(2)}) %collective-permute-start.2) | collective-permute-done | bytes 786464 | tf_op jit(solution)/shard_map/ppermute | solution.py:24
  190.0 1.5 collective-permute-start.5
  191.9 1.5 collective-permute-start.3
  193.7 6.4 %collective-permute-done.11 = bf16[192,1024]{1,0:T(8,128)(2,1)S(1)} collective-permute-done((bf16[192,1024]{1,0:T(8,128)(2,1)S(1)}, bf16[192,1024]{1,0:T(8,128)(2,1)S(1)}, u32[]{:S(2)}, u32[]{:S(2)}) %collective-permute-start.11) | collective-permute-done | bytes 393248 | tf_op jit(solution)/shard_map/ppermute | solution.py:24
  200.9 0.9 maximum_bitcast_fusion.2
  201.9 6.7 %collective-permute-done.7 = bf16[192,1024]{1,0:T(8,128)(2,1)S(1)} collective-permute-done((bf16[192,1024]{1,0:T(8,128)(2,1)S(1)}, bf16[192,1024]{1,0:T(8,128)(2,1)S(1)}, u32[]{:S(2)}, u32[]{:S(2)}) %collective-permute-start.7) | collective-permute-done | bytes 393248 | tf_op jit(solution)/shard_map/ppermute | solution.py:24
  209.8 6.2 %collective-permute-done.3 = bf16[192,1024]{1,0:T(8,128)(2,1)S(1)} collective-permute-done((bf16[192,1024]{1,0:T(8,128)(2,1)S(1)}, bf16[192,1024]{1,0:T(8,128)(2,1)S(1)}, u32[]{:S(2)}, u32[]{:S(2)}) %collective-permute-start.3) | collective-permute-done | bytes 393248 | tf_op jit(solution)/shard_map/ppermute | solution.py:24
  218.7 1.9 slice.60
  (91 shorter events, 15.6 us)
Async XLA Ops:
  7.2 104.9 %copy-start = (bf16[1,768,2048]{2,1,0:T(8,128)(2,1)S(1)}, bf16[1,768,2048]{2,1,0:T(8,128)(2,1)}, u32[]{:S(2)}) copy-start(bf16[1,768,2048]{2,1,0:T(8,128)(2,1)} %param.13) | copy-start | bytes 9437188
  7.2 52.3 %all-gather.6.cloned.1.call-start = ((), (), s32[]{:S(2)}) async-start(), calls=%async_computation.2 | async-start | bytes 4718592 | tf_op jit(solution)/shard_map/all_gather | solution.py:51
  7.9 99.1 %all-gather.4.cloned.1.call-start = ((), (), s32[]{:S(2)}) async-start(), calls=%async_computation.1 | async-start | bytes 4718592 | tf_op jit(solution)/shard_map/all_gather | solution.py:52
  8.7 208.5 %reduce-scatter.2.cloned.1.call-start = ((), (), s32[]{:S(2)}) async-start(), calls=%async_computation.3 | async-start | bytes 5013504 | tf_op jit(solution)/shard_map/reduce_scatter | solution.py:99
  59.5 6.6 %copy-start.3 = (bf16[1,2048,768]{2,1,0:T(8,128)(2,1)S(1)}, bf16[1,2048,768]{2,1,0:T(8,128)(2,1)}, u32[]{:S(2)}) copy-start(bf16[1,2048,768]{2,1,0:T(8,128)(2,1)} %param.12) | copy-start | bytes 9437188
  64.7 1.4 copy-start.6
  112.1 2.1 copy-start.10
  112.1 2.7 %copy-start.5 = (bf16[1,2048,768]{2,1,0:T(8,128)(2,1)S(1)}, bf16[1,2048,768]{2,1,0:T(8,128)(2,1)}, u32[]{:S(2)}) copy-start(bf16[1,2048,768]{2,1,0:T(8,128)(2,1)} %param.11) | copy-start | bytes 9437188
  112.1 3.5 %copy-start.7 = (bf16[576,2048]{1,0:T(8,128)(2,1)S(1)}, bf16[576,2048]{1,0:T(8,128)(2,1)}, u32[]{:S(2)}) copy-start(bf16[576,2048]{1,0:T(8,128)(2,1)} %copy-done.6) | copy-start | bytes 7077892
  112.1 3.9 %copy-start.9 = (f32[576,768]{1,0:T(8,128)S(1)}, f32[576,768]{1,0:T(8,128)}, u32[]{:S(2)}) copy-start(f32[576,768]{1,0:T(8,128)} %fusion.38) | copy-start | bytes 5308420
  116.0 4.1 %copy-start.4 = (bf16[1,2048,768]{2,1,0:T(8,128)(2,1)S(1)}, bf16[1,2048,768]{2,1,0:T(8,128)(2,1)}, u32[]{:S(2)}) copy-start(bf16[1,2048,768]{2,1,0:T(8,128)(2,1)} %param.12) | copy-start | bytes 9437188
  119.9 4.1 %copy-start.11 = (bf16[576,768]{1,0:T(8,128)(2,1)}, bf16[576,768]{1,0:T(8,128)(2,1)S(1)}, u32[]{:S(2)}) copy-start(bf16[576,768]{1,0:T(8,128)(2,1)S(1)} %get-tuple-element.7) | copy-start | bytes 2654212
  119.9 4.1 %copy-start.13 = (bf16[576,768]{1,0:T(8,128)(2,1)}, bf16[576,768]{1,0:T(8,128)(2,1)S(1)}, u32[]{:S(2)}) copy-start(bf16[576,768]{1,0:T(8,128)(2,1)S(1)} %get-tuple-element.9) | copy-start | bytes 2654212
  135.4 3.6 %copy-start.14 = (bf16[576,768]{1,0:T(8,128)(2,1)S(1)}, bf16[576,768]{1,0:T(8,128)(2,1)}, u32[]{:S(2)}) copy-start(bf16[576,768]{1,0:T(8,128)(2,1)} %copy-done.13) | copy-start | bytes 2654212
  135.8 3.2 %copy-start.8 = (bf16[576,2048]{1,0:T(8,128)(2,1)S(1)}, bf16[576,2048]{1,0:T(8,128)(2,1)}, u32[]{:S(2)}) copy-start(bf16[576,2048]{1,0:T(8,128)(2,1)} %copy-done.6) | copy-start | bytes 7077892
  135.9 20.4 %collective-permute-start.10 = (bf16[2,192,1024]{2,1,0:T(8,128)(2,1)S(1)}, bf16[2,192,1024]{2,1,0:T(8,128)(2,1)S(1)}, u32[]{:S(2)}, u32[]{:S(2)}) collective-permute-start(bf16[2,192,1024]{2,1,0:T(8,128)(2,1)S(1)} %dynamic-slice_bitcast_fusion), channel_id=1, source_target_pairs={{0,16},{8,24},{16,0},{24,8},{1,17},{9,25},{17,1},{25,9},{2,18},{10... | collective-permute-start | bytes 2359304 | tf_op jit(solution)/shard_map/ppermute | solution.py:24
  137.5 20.7 %collective-permute-start.8 = (bf16[2,192,1024]{2,1,0:T(8,128)(2,1)S(1)}, bf16[2,192,1024]{2,1,0:T(8,128)(2,1)S(1)}, u32[]{:S(2)}, u32[]{:S(2)}) collective-permute-start(bf16[2,192,1024]{2,1,0:T(8,128)(2,1)S(1)} %dynamic-slice_bitcast_fusion.1), channel_id=1, source_target_pairs={{0,8},{8,0},{16,24},{24,16},{1,9},{9,1},{17,25},{25,17},{2,10},{10... | collective-permute-start | bytes 2359304 | tf_op jit(solution)/shard_map/ppermute | solution.py:24
  141.9 1.2 copy-start.12
  146.6 26.6 %collective-permute-start.6 = (bf16[2,192,1024]{2,1,0:T(8,128)(2,1)S(1)}, bf16[2,192,1024]{2,1,0:T(8,128)(2,1)S(1)}, u32[]{:S(2)}, u32[]{:S(2)}) collective-permute-start(bf16[2,192,1024]{2,1,0:T(8,128)(2,1)S(1)} %dynamic-slice_bitcast_fusion.2), channel_id=1, source_target_pairs={{0,16},{8,24},{16,0},{24,8},{1,17},{9,25},{17,1},{25,9},{2,18},{10... | collective-permute-start | bytes 2359304 | tf_op jit(solution)/shard_map/ppermute | solution.py:24
  147.4 27.7 %collective-permute-start.4 = (bf16[2,192,1024]{2,1,0:T(8,128)(2,1)S(1)}, bf16[2,192,1024]{2,1,0:T(8,128)(2,1)S(1)}, u32[]{:S(2)}, u32[]{:S(2)}) collective-permute-start(bf16[2,192,1024]{2,1,0:T(8,128)(2,1)S(1)} %dynamic-slice_bitcast_fusion.3), channel_id=1, source_target_pairs={{0,8},{8,0},{16,24},{24,16},{1,9},{9,1},{17,25},{25,17},{2,10},{10... | collective-permute-start | bytes 2359304 | tf_op jit(solution)/shard_map/ppermute | solution.py:24
  148.3 41.7 %collective-permute-start.2 = (bf16[2,192,1024]{2,1,0:T(8,128)(2,1)S(1)}, bf16[2,192,1024]{2,1,0:T(8,128)(2,1)S(1)}, u32[]{:S(2)}, u32[]{:S(2)}) collective-permute-start(bf16[2,192,1024]{2,1,0:T(8,128)(2,1)S(1)} %dynamic-slice_bitcast_fusion.4), channel_id=1, source_target_pairs={{0,16},{8,24},{16,0},{24,8},{1,17},{9,25},{17,1},{25,9},{2,18},{10... | collective-permute-start | bytes 2359304 | tf_op jit(solution)/shard_map/ppermute | solution.py:24
  156.3 35.6 %collective-permute-start = (bf16[2,192,1024]{2,1,0:T(8,128)(2,1)S(1)}, bf16[2,192,1024]{2,1,0:T(8,128)(2,1)S(1)}, u32[]{:S(2)}, u32[]{:S(2)}) collective-permute-start(bf16[2,192,1024]{2,1,0:T(8,128)(2,1)S(1)} %dynamic-slice_bitcast_fusion.5), channel_id=1, source_target_pairs={{0,8},{8,0},{16,24},{24,16},{1,9},{9,1},{17,25},{25,17},{2,10},{10... | collective-permute-start | bytes 2359304 | tf_op jit(solution)/shard_map/ppermute | solution.py:24
  158.1 41.9 %collective-permute-start.11 = (bf16[192,1024]{1,0:T(8,128)(2,1)S(1)}, bf16[192,1024]{1,0:T(8,128)(2,1)S(1)}, u32[]{:S(2)}, u32[]{:S(2)}) collective-permute-start(bf16[192,1024]{1,0:T(8,128)(2,1)S(1)} %dynamic-slice_bitcast_fusion.6), channel_id=1, source_target_pairs={{0,8},{8,0},{16,24},{24,16},{1,9},{9,1},{17,25},{25,17},{2,10},{10... | collective-permute-start | bytes 1179656 | tf_op jit(solution)/shard_map/ppermute | solution.py:24
  173.2 27.6 %collective-permute-start.9 = (bf16[192,1024]{1,0:T(8,128)(2,1)S(1)}, bf16[192,1024]{1,0:T(8,128)(2,1)S(1)}, u32[]{:S(2)}, u32[]{:S(2)}) collective-permute-start(bf16[192,1024]{1,0:T(8,128)(2,1)S(1)} %dynamic-slice_bitcast_fusion.7), channel_id=1, source_target_pairs={{0,16},{8,24},{16,0},{24,8},{1,17},{9,25},{17,1},{25,9},{2,18},{10... | collective-permute-start | bytes 1179656 | tf_op jit(solution)/shard_map/ppermute | solution.py:24
  175.0 33.5 %collective-permute-start.7 = (bf16[192,1024]{1,0:T(8,128)(2,1)S(1)}, bf16[192,1024]{1,0:T(8,128)(2,1)S(1)}, u32[]{:S(2)}, u32[]{:S(2)}) collective-permute-start(bf16[192,1024]{1,0:T(8,128)(2,1)S(1)} %dynamic-slice_bitcast_fusion.8), channel_id=1, source_target_pairs={{0,8},{8,0},{16,24},{24,16},{1,9},{9,1},{17,25},{25,17},{2,10},{10... | collective-permute-start | bytes 1179656 | tf_op jit(solution)/shard_map/ppermute | solution.py:24
  190.0 18.7 %collective-permute-start.5 = (bf16[192,1024]{1,0:T(8,128)(2,1)S(1)}, bf16[192,1024]{1,0:T(8,128)(2,1)S(1)}, u32[]{:S(2)}, u32[]{:S(2)}) collective-permute-start(bf16[192,1024]{1,0:T(8,128)(2,1)S(1)} %dynamic-slice_bitcast_fusion.9), channel_id=1, source_target_pairs={{0,16},{8,24},{16,0},{24,8},{1,17},{9,25},{17,1},{25,9},{2,18},{10... | collective-permute-start | bytes 1179656 | tf_op jit(solution)/shard_map/ppermute | solution.py:24
  191.9 24.1 %collective-permute-start.3 = (bf16[192,1024]{1,0:T(8,128)(2,1)S(1)}, bf16[192,1024]{1,0:T(8,128)(2,1)S(1)}, u32[]{:S(2)}, u32[]{:S(2)}) collective-permute-start(bf16[192,1024]{1,0:T(8,128)(2,1)S(1)} %dynamic-slice_bitcast_fusion.10), channel_id=1, source_target_pairs={{0,8},{8,0},{16,24},{24,16},{1,9},{9,1},{17,25},{25,17},{2,10},{10... | collective-permute-start | bytes 1179656 | tf_op jit(solution)/shard_map/ppermute | solution.py:24
  200.1 16.0 %collective-permute-start.1 = (bf16[192,1024]{1,0:T(8,128)(2,1)S(1)}, bf16[192,1024]{1,0:T(8,128)(2,1)S(1)}, u32[]{:S(2)}, u32[]{:S(2)}) collective-permute-start(bf16[192,1024]{1,0:T(8,128)(2,1)S(1)} %dynamic-slice_bitcast_fusion.11), channel_id=1, source_target_pairs={{0,16},{8,24},{16,0},{24,8},{1,17},{9,25},{17,1},{25,9},{2,18},{10... | collective-permute-start | bytes 1179656 | tf_op jit(solution)/shard_map/ppermute | solution.py:24
  209.8 8.3 %copy-start.2 = (s32[128,4]{0,1:T(4,128)S(1)}, s32[128,4]{0,1:T(4,128)}, u32[]{:S(2)}) copy-start(s32[128,4]{0,1:T(4,128)} %param.10) | copy-start | bytes 6148
  215.9 4.7 %copy-start.1 = (bf16[1,768,2048]{2,1,0:T(8,128)(2,1)S(1)}, bf16[1,768,2048]{2,1,0:T(8,128)(2,1)}, u32[]{:S(2)}) copy-start(bf16[1,768,2048]{2,1,0:T(8,128)(2,1)} %param.13) | copy-start | bytes 9437188
Sparse Core Ops, SparseCore 0:
  9.6 49.8 all-gather.5
  61.1 45.9 all-gather.3
  129.9 51.1 reduce-scatter.1

commit v3 on v2

--- a/solution.py
+++ b/solution.py
@@ -81,10 +81,12 @@
     grad_up = (scaled_hidden * silu).astype(jnp.bfloat16)
     scaled_dy = (prob_slots * dy_slots.astype(jnp.float32)).astype(jnp.bfloat16)
 
-    down_sum = dp_sum(outer_rows(hidden, scaled_dy).astype(jnp.bfloat16))
+    down_term = outer_rows(hidden, scaled_dy).astype(jnp.bfloat16)
+    down_term, row_gate = lax.optimization_barrier((down_term, grad_gate))
+    down_sum = dp_sum(down_term)
 
     row_grad = rows_dot(
-        jnp.concatenate([grad_gate, grad_up], axis=1),
+        jnp.concatenate([row_gate, grad_up], axis=1),
         jnp.concatenate([gate_mat, up_mat], axis=1),
     ).astype(jnp.bfloat16)
     prob_high = lax.reduce_precision(prob_grad, 8, 7)

time: 227 us -> 223 us (0.982)
  matrix products: 40.3 us -> 37.2 us
    dot_general x4, matrix products: 17.3 us -> 15 us  [outer_rows(): lax.dot_general(left, right, (((0,), (0,)), ((), ())), preferred_element_...]
  transfers between devices with their start and end apart: 15 -> 15, of which waited for: 8 -> 8; matrix products, arithmetic and copies ran while one was open for 13% -> 11% of each run, Pallas kernels for 0% -> 0%
where the time goes in v3:
time: 223 us
  waiting for transfers between devices  126 us (57%)
  matrix products  37.2 us (17%)
  starting transfers between devices  15.2 us (7%)
  blocking collectives  14.4 us (6%)
  between operations  14.3 us (6%)
  other arithmetic  9.29 us (4%)
  local copies, waits for them, and re-layouts  6.98 us (3%)
    ppermute x12, waiting for transfers between devices, halve(): got = lax.ppermute(give, 'dp', [(d, d ^ bit) for d in range(n_dp)])  52.5 us
    all_gather x1, waiting for transfers between devices, per_device(): dy_all = lax.all_gather(out_grad, 'expert', axis=0, tiled=True)  37.6 us
    all_gather x1, waiting for transfers between devices, per_device(): x_all = lax.all_gather(tokens, 'expert', axis=0, tiled=True)  34.1 us
    ppermute x12, starting transfers between devices, halve(): got = lax.ppermute(give, 'dp', [(d, d ^ bit) for d in range(n_dp)])  15.1 us
    dot_general x4, matrix products, outer_rows(): lax.dot_general(left, right, (((0,), (0,)), ((), ())), preferred_element_...  15 us
    all_gather x1, blocking collectives, per_device(): routes = lax.all_gather(route, 'expert', axis=0, tiled=False)  14.4 us
    dot_general x2, matrix products, rows_dot(): lax.dot_general(left, right, (((1,), (1,)), ((), ())), preferred_element_...  5.96 us
    dot_general x1, matrix products, per_device(): jnp.dot(pick, x_all, preferred_element_type=jnp.float32)  5.14 us
  transfers between devices with their start and end apart: 15, of which 8 were waited for; matrix products, arithmetic and copies ran while one was open for 11% of the time, Pallas kernels for 0%

profile of v3, /device:TPU:0, one launch (start us, length us, event | category | flops | bytes accessed | tf_op | source)
XLA Modules:
  0.0 223.0 jit_solution(16969952979193529504)
XLA Ops:
  10.1 14.4 %all-gather = bf16[64,128]{1,0:T(8,128)(2,1)S(1)} all-gather(bf16[8,128]{1,0:T(8,128)(2,1)S(1)} %maximum_bitcast_fusion.3), channel_id=2, replica_groups=mesh['dp'=4,'expert'=8] {'expert'}, dimensions={0}, use_global_device_ids=true | all-gather | bytes 18432 | tf_op jit(solution)/shard_map/all_gather | solution.py:50
  25.4 34.1 %all-gather.4.cloned.1.call-done = bf16[1024,2048]{1,0:T(8,128)(2,1)} async-done(((bf16[128,2048]{1,0:T(8,128)(2,1)}), bf16[1024,2048]{1,0:T(8,128)(2,1)}) %all-gather.4.cloned.1.call-update) | async-done | bytes 4194320 | tf_op jit(solution)/shard_map/all_gather | solution.py:51
  59.5 5.1 %convolution_convert_fusion.5 = bf16[576,2048]{1,0:T(8,128)(2,1)S(1)} fusion(bf16[1024,2048]{1,0:T(8,128)(2,1)} %all-gather.4.cloned.1.call-done, s32[1024]{0:T(1024)S(1)} %select_bitcast_fusion), kind=kOutput, calls=%fused_computation.13 | convolution fusion | flops 2417688576 | bytes 6557696 | tf_op jit(solution)/shard_map/dot_general | solution.py:66
  64.7 1.4 copy-done.6
  66.1 3.3 %fusion.36 = f32[576,768]{1,0:T(8,128)} fusion(bf16[576,2048]{1,0:T(8,128)(2,1)S(1)} %convolution_convert_fusion.5, bf16[1,2048,768]{2,1,0:T(8,128)(2,1)S(1)} %copy-done.3), kind=kOutput, calls=%fused_computation.87 | convolution fusion | flops 1811939328 | bytes 7274496 | tf_op jit(solution)/shard_map/dot_general | solution.py:68
  69.4 37.6 %all-gather.6.cloned.1.call-done = bf16[1024,2048]{1,0:T(8,128)(2,1)} async-done(((bf16[128,2048]{1,0:T(8,128)(2,1)}), bf16[1024,2048]{1,0:T(8,128)(2,1)}) %all-gather.6.cloned.1.call-update) | async-done | bytes 4194320 | tf_op jit(solution)/shard_map/all_gather | solution.py:52
  107.0 5.0 %convolution_convert_fusion.4 = bf16[576,2048]{1,0:T(8,128)(2,1)S(1)} fusion(bf16[1024,2048]{1,0:T(8,128)(2,1)} %all-gather.6.cloned.1.call-done, s32[1024]{0:T(1024)S(1)} %select_bitcast_fusion), kind=kOutput, calls=%fused_computation.12 | convolution fusion | flops 2417688576 | bytes 6557696 | tf_op jit(solution)/shard_map/dot_general | solution.py:74
  112.1 2.1 fusion.4
  115.2 2.9 %multiply_convert_fusion.3 = (bf16[576,768]{1,0:T(8,128)(2,1)S(1)}, f32[576]{0:T(1024)S(1)}, bf16[576,768]{1,0:T(8,128)(2,1)S(1)}, f32[576,768]{1,0:T(8,128)S(1)}) fusion(f32[576,768]{1,0:T(8,128)S(1)} %copy-done.9, f32[576,768]{1,0:T(8,128)S(1)} %fusion.4, f32[576]{0:T(1024)S(1)} %select_reduce_fusion, bf16[576,2048]{1,0:T(8,128)(2,1)S(1)} %copy-done.7, ...), kind=kOutput, calls=%fused_computation.25 | convolution fusion | flops 1819459072 | bytes 12587520 | tf_op jit(solution)/shard_map/dot_general | solution.py:67
  118.1 3.4 %convolution_convert_fusion.3 = bf16[768,2048]{1,0:T(8,128)(2,1)S(1)} fusion(bf16[576,2048]{1,0:T(8,128)(2,1)S(1)} %convolution_convert_fusion.4, f32[576]{0:T(1024)S(1)} %select_reduce_fusion, f32[576,768]{1,0:T(8,128)S(1)} %copy-done.9, f32[576,768]{1,0:T(8,128)S(1)} %get-tuple-element.22), kind=kOutput, calls=%fused_computation.8 | convolution fusion | flops 1819705344 | bytes 9046272 | tf_op jit(solution)/shard_map/dot_general | solution.py:14
  121.8 3.8 %fusion.6 = bf16[576,2048]{1,0:T(8,128)(2,1)S(1)} fusion(bf16[2048,768]{1,0:T(8,128)(2,1)S(1)} %bitcast.105, bf16[2048,768]{1,0:T(8,128)(2,1)S(1)} %bitcast.106, bf16[576,768]{1,0:T(8,128)(2,1)S(1)} %get-tuple-element.13, bf16[576,768]{1,0:T(8,128)(2,1)S(1)} %get-tuple-element.8), kind=kOutput, calls=%fused_computation.11 | convolution fusion | flops 3641180160 | bytes 10420224 | tf_op jit(solution)/shard_map/dot_general | solution.py:8
  125.7 5.6 %convolution_convert_fusion = bf16[1024,2176]{1,0:T(8,128)(2,1)} fusion(bf16[576,128]{1,0:T(8,128)(2,1)S(1)} %add_convert_fusion, bf16[576,2048]{1,0:T(8,128)(2,1)S(1)} %fusion.6, s32[1024]{0:T(1024)S(1)} %select_bitcast_fusion), kind=kOutput, calls=%fused_computation.4 | convolution fusion | flops 2574745600 | bytes 6967296 | tf_op jit(solution)/shard_map/dot_general | solution.py:14
  131.8 1.6 collective-permute-start.10
  133.4 1.5 collective-permute-start.8
  134.9 2.9 %convolution_convert_fusion.1 = bf16[768,2048]{1,0:T(8,128)(2,1)S(1)} fusion(bf16[576,768]{1,0:T(8,128)(2,1)S(1)} %copy-done.13, bf16[576,2048]{1,0:T(8,128)(2,1)S(1)} %copy-done.8), kind=kOutput, calls=%fused_computation.6 | convolution fusion | flops 1813512192 | bytes 6389760 | tf_op jit(solution)/shard_map/dot_general | solution.py:14
  139.0 3.1 %convolution_convert_fusion.2 = bf16[768,2048]{1,0:T(8,128)(2,1)S(1)} fusion(bf16[576,768]{1,0:T(8,128)(2,1)S(1)} %copy-done.11, bf16[576,2048]{1,0:T(8,128)(2,1)S(1)} %copy-done.8), kind=kOutput, calls=%fused_computation.7 | convolution fusion | flops 1813512192 | bytes 6389760 | tf_op jit(solution)/shard_map/dot_general | solution.py:14
  143.3 1.0 collective-permute-start.4
  144.3 1.1 collective-permute-start.2
  145.4 6.8 %collective-permute-done.10 = bf16[2,192,1024]{2,1,0:T(8,128)(2,1)S(1)} collective-permute-done((bf16[2,192,1024]{2,1,0:T(8,128)(2,1)S(1)}, bf16[2,192,1024]{2,1,0:T(8,128)(2,1)S(1)}, u32[]{:S(2)}, u32[]{:S(2)}) %collective-permute-start.10) | collective-permute-done | bytes 786464 | tf_op jit(solution)/shard_map/ppermute | solution.py:24
  152.2 1.5 collective-permute-start
  154.1 1.3 collective-permute-start.11
  155.7 13.4 %collective-permute-done.6 = bf16[2,192,1024]{2,1,0:T(8,128)(2,1)S(1)} collective-permute-done((bf16[2,192,1024]{2,1,0:T(8,128)(2,1)S(1)}, bf16[2,192,1024]{2,1,0:T(8,128)(2,1)S(1)}, u32[]{:S(2)}, u32[]{:S(2)}) %collective-permute-start.6) | collective-permute-done | bytes 786464 | tf_op jit(solution)/shard_map/ppermute | solution.py:24
  169.1 1.5 collective-permute-start.9
  170.9 1.5 collective-permute-start.7
  172.8 13.1 %collective-permute-done.2 = bf16[2,192,1024]{2,1,0:T(8,128)(2,1)S(1)} collective-permute-done((bf16[2,192,1024]{2,1,0:T(8,128)(2,1)S(1)}, bf16[2,192,1024]{2,1,0:T(8,128)(2,1)S(1)}, u32[]{:S(2)}, u32[]{:S(2)}) %collective-permute-start.2) | collective-permute-done | bytes 786464 | tf_op jit(solution)/shard_map/ppermute | solution.py:24
  185.9 1.5 collective-permute-start.5
  187.8 1.5 collective-permute-start.3
  189.6 6.4 %collective-permute-done.11 = bf16[192,1024]{1,0:T(8,128)(2,1)S(1)} collective-permute-done((bf16[192,1024]{1,0:T(8,128)(2,1)S(1)}, bf16[192,1024]{1,0:T(8,128)(2,1)S(1)}, u32[]{:S(2)}, u32[]{:S(2)}) %collective-permute-start.11) | collective-permute-done | bytes 393248 | tf_op jit(solution)/shard_map/ppermute | solution.py:24
  196.8 0.9 maximum_bitcast_fusion.2
  197.8 6.7 %collective-permute-done.7 = bf16[192,1024]{1,0:T(8,128)(2,1)S(1)} collective-permute-done((bf16[192,1024]{1,0:T(8,128)(2,1)S(1)}, bf16[192,1024]{1,0:T(8,128)(2,1)S(1)}, u32[]{:S(2)}, u32[]{:S(2)}) %collective-permute-start.7) | collective-permute-done | bytes 393248 | tf_op jit(solution)/shard_map/ppermute | solution.py:24
  205.7 6.2 %collective-permute-done.3 = bf16[192,1024]{1,0:T(8,128)(2,1)S(1)} collective-permute-done((bf16[192,1024]{1,0:T(8,128)(2,1)S(1)}, bf16[192,1024]{1,0:T(8,128)(2,1)S(1)}, u32[]{:S(2)}, u32[]{:S(2)}) %collective-permute-start.3) | collective-permute-done | bytes 393248 | tf_op jit(solution)/shard_map/ppermute | solution.py:24
  214.6 1.9 slice.60
  (89 shorter events, 14.7 us)
Async XLA Ops:
  7.2 104.9 %copy-start = (bf16[1,768,2048]{2,1,0:T(8,128)(2,1)S(1)}, bf16[1,768,2048]{2,1,0:T(8,128)(2,1)}, u32[]{:S(2)}) copy-start(bf16[1,768,2048]{2,1,0:T(8,128)(2,1)} %param.13) | copy-start | bytes 9437188
  7.2 52.3 %all-gather.4.cloned.1.call-start = ((), (), s32[]{:S(2)}) async-start(), calls=%async_computation.1 | async-start | bytes 4718592 | tf_op jit(solution)/shard_map/all_gather | solution.py:51
  7.9 99.1 %all-gather.6.cloned.1.call-start = ((), (), s32[]{:S(2)}) async-start(), calls=%async_computation.2 | async-start | bytes 4718592 | tf_op jit(solution)/shard_map/all_gather | solution.py:52
  8.7 204.4 %reduce-scatter.2.cloned.1.call-start = ((), (), s32[]{:S(2)}) async-start(), calls=%async_computation.3 | async-start | bytes 5013504 | tf_op jit(solution)/shard_map/reduce_scatter | solution.py:101
  59.5 6.6 %copy-start.3 = (bf16[1,2048,768]{2,1,0:T(8,128)(2,1)S(1)}, bf16[1,2048,768]{2,1,0:T(8,128)(2,1)}, u32[]{:S(2)}) copy-start(bf16[1,2048,768]{2,1,0:T(8,128)(2,1)} %param.12) | copy-start | bytes 9437188
  64.7 1.5 copy-start.6
  112.1 2.2 copy-start.5
  112.1 2.6 %copy-start.7 = (bf16[576,2048]{1,0:T(8,128)(2,1)S(1)}, bf16[576,2048]{1,0:T(8,128)(2,1)}, u32[]{:S(2)}) copy-start(bf16[576,2048]{1,0:T(8,128)(2,1)} %copy-done.6) | copy-start | bytes 7077892
  112.1 3.1 %copy-start.9 = (f32[576,768]{1,0:T(8,128)S(1)}, f32[576,768]{1,0:T(8,128)}, u32[]{:S(2)}) copy-start(f32[576,768]{1,0:T(8,128)} %fusion.36) | copy-start | bytes 5308420
  118.1 3.7 %copy-start.10 = (bf16[576,768]{1,0:T(8,128)(2,1)}, bf16[576,768]{1,0:T(8,128)(2,1)S(1)}, u32[]{:S(2)}) copy-start(bf16[576,768]{1,0:T(8,128)(2,1)S(1)} %get-tuple-element.8) | copy-start | bytes 2654212
  118.1 3.7 %copy-start.12 = (bf16[576,768]{1,0:T(8,128)(2,1)}, bf16[576,768]{1,0:T(8,128)(2,1)S(1)}, u32[]{:S(2)}) copy-start(bf16[576,768]{1,0:T(8,128)(2,1)S(1)} %get-tuple-element.13) | copy-start | bytes 2654212
  118.1 3.7 %copy-start.4 = (bf16[1,2048,768]{2,1,0:T(8,128)(2,1)S(1)}, bf16[1,2048,768]{2,1,0:T(8,128)(2,1)}, u32[]{:S(2)}) copy-start(bf16[1,2048,768]{2,1,0:T(8,128)(2,1)} %param.12) | copy-start | bytes 9437188
  131.3 3.6 %copy-start.13 = (bf16[576,768]{1,0:T(8,128)(2,1)S(1)}, bf16[576,768]{1,0:T(8,128)(2,1)}, u32[]{:S(2)}) copy-start(bf16[576,768]{1,0:T(8,128)(2,1)} %copy-done.12) | copy-start | bytes 2654212
  131.7 3.2 %copy-start.8 = (bf16[576,2048]{1,0:T(8,128)(2,1)S(1)}, bf16[576,2048]{1,0:T(8,128)(2,1)}, u32[]{:S(2)}) copy-start(bf16[576,2048]{1,0:T(8,128)(2,1)} %copy-done.6) | copy-start | bytes 7077892
  131.8 20.4 %collective-permute-start.10 = (bf16[2,192,1024]{2,1,0:T(8,128)(2,1)S(1)}, bf16[2,192,1024]{2,1,0:T(8,128)(2,1)S(1)}, u32[]{:S(2)}, u32[]{:S(2)}) collective-permute-start(bf16[2,192,1024]{2,1,0:T(8,128)(2,1)S(1)} %dynamic-slice_bitcast_fusion), channel_id=1, source_target_pairs={{0,16},{8,24},{16,0},{24,8},{1,17},{9,25},{17,1},{25,9},{2,18},{10... | collective-permute-start | bytes 2359304 | tf_op jit(solution)/shard_map/ppermute | solution.py:24
  133.4 20.7 %collective-permute-start.8 = (bf16[2,192,1024]{2,1,0:T(8,128)(2,1)S(1)}, bf16[2,192,1024]{2,1,0:T(8,128)(2,1)S(1)}, u32[]{:S(2)}, u32[]{:S(2)}) collective-permute-start(bf16[2,192,1024]{2,1,0:T(8,128)(2,1)S(1)} %dynamic-slice_bitcast_fusion.1), channel_id=1, source_target_pairs={{0,8},{8,0},{16,24},{24,16},{1,9},{9,1},{17,25},{25,17},{2,10},{10... | collective-permute-start | bytes 2359304 | tf_op jit(solution)/shard_map/ppermute | solution.py:24
  137.8 1.2 copy-start.11
  142.5 26.6 %collective-permute-start.6 = (bf16[2,192,1024]{2,1,0:T(8,128)(2,1)S(1)}, bf16[2,192,1024]{2,1,0:T(8,128)(2,1)S(1)}, u32[]{:S(2)}, u32[]{:S(2)}) collective-permute-start(bf16[2,192,1024]{2,1,0:T(8,128)(2,1)S(1)} %dynamic-slice_bitcast_fusion.2), channel_id=1, source_target_pairs={{0,16},{8,24},{16,0},{24,8},{1,17},{9,25},{17,1},{25,9},{2,18},{10... | collective-permute-start | bytes 2359304 | tf_op jit(solution)/shard_map/ppermute | solution.py:24
  143.3 27.6 %collective-permute-start.4 = (bf16[2,192,1024]{2,1,0:T(8,128)(2,1)S(1)}, bf16[2,192,1024]{2,1,0:T(8,128)(2,1)S(1)}, u32[]{:S(2)}, u32[]{:S(2)}) collective-permute-start(bf16[2,192,1024]{2,1,0:T(8,128)(2,1)S(1)} %dynamic-slice_bitcast_fusion.3), channel_id=1, source_target_pairs={{0,8},{8,0},{16,24},{24,16},{1,9},{9,1},{17,25},{25,17},{2,10},{10... | collective-permute-start | bytes 2359304 | tf_op jit(solution)/shard_map/ppermute | solution.py:24
  144.3 41.6 %collective-permute-start.2 = (bf16[2,192,1024]{2,1,0:T(8,128)(2,1)S(1)}, bf16[2,192,1024]{2,1,0:T(8,128)(2,1)S(1)}, u32[]{:S(2)}, u32[]{:S(2)}) collective-permute-start(bf16[2,192,1024]{2,1,0:T(8,128)(2,1)S(1)} %dynamic-slice_bitcast_fusion.4), channel_id=1, source_target_pairs={{0,16},{8,24},{16,0},{24,8},{1,17},{9,25},{17,1},{25,9},{2,18},{10... | collective-permute-start | bytes 2359304 | tf_op jit(solution)/shard_map/ppermute | solution.py:24
  152.2 35.6 %collective-permute-start = (bf16[2,192,1024]{2,1,0:T(8,128)(2,1)S(1)}, bf16[2,192,1024]{2,1,0:T(8,128)(2,1)S(1)}, u32[]{:S(2)}, u32[]{:S(2)}) collective-permute-start(bf16[2,192,1024]{2,1,0:T(8,128)(2,1)S(1)} %dynamic-slice_bitcast_fusion.5), channel_id=1, source_target_pairs={{0,8},{8,0},{16,24},{24,16},{1,9},{9,1},{17,25},{25,17},{2,10},{10... | collective-permute-start | bytes 2359304 | tf_op jit(solution)/shard_map/ppermute | solution.py:24
  154.1 41.9 %collective-permute-start.11 = (bf16[192,1024]{1,0:T(8,128)(2,1)S(1)}, bf16[192,1024]{1,0:T(8,128)(2,1)S(1)}, u32[]{:S(2)}, u32[]{:S(2)}) collective-permute-start(bf16[192,1024]{1,0:T(8,128)(2,1)S(1)} %dynamic-slice_bitcast_fusion.6), channel_id=1, source_target_pairs={{0,8},{8,0},{16,24},{24,16},{1,9},{9,1},{17,25},{25,17},{2,10},{10... | collective-permute-start | bytes 1179656 | tf_op jit(solution)/shard_map/ppermute | solution.py:24
  169.1 27.6 %collective-permute-start.9 = (bf16[192,1024]{1,0:T(8,128)(2,1)S(1)}, bf16[192,1024]{1,0:T(8,128)(2,1)S(1)}, u32[]{:S(2)}, u32[]{:S(2)}) collective-permute-start(bf16[192,1024]{1,0:T(8,128)(2,1)S(1)} %dynamic-slice_bitcast_fusion.7), channel_id=1, source_target_pairs={{0,16},{8,24},{16,0},{24,8},{1,17},{9,25},{17,1},{25,9},{2,18},{10... | collective-permute-start | bytes 1179656 | tf_op jit(solution)/shard_map/ppermute | solution.py:24
  170.9 33.5 %collective-permute-start.7 = (bf16[192,1024]{1,0:T(8,128)(2,1)S(1)}, bf16[192,1024]{1,0:T(8,128)(2,1)S(1)}, u32[]{:S(2)}, u32[]{:S(2)}) collective-permute-start(bf16[192,1024]{1,0:T(8,128)(2,1)S(1)} %dynamic-slice_bitcast_fusion.8), channel_id=1, source_target_pairs={{0,8},{8,0},{16,24},{24,16},{1,9},{9,1},{17,25},{25,17},{2,10},{10... | collective-permute-start | bytes 1179656 | tf_op jit(solution)/shard_map/ppermute | solution.py:24
  185.9 18.7 %collective-permute-start.5 = (bf16[192,1024]{1,0:T(8,128)(2,1)S(1)}, bf16[192,1024]{1,0:T(8,128)(2,1)S(1)}, u32[]{:S(2)}, u32[]{:S(2)}) collective-permute-start(bf16[192,1024]{1,0:T(8,128)(2,1)S(1)} %dynamic-slice_bitcast_fusion.9), channel_id=1, source_target_pairs={{0,16},{8,24},{16,0},{24,8},{1,17},{9,25},{17,1},{25,9},{2,18},{10... | collective-permute-start | bytes 1179656 | tf_op jit(solution)/shard_map/ppermute | solution.py:24
  187.8 24.1 %collective-permute-start.3 = (bf16[192,1024]{1,0:T(8,128)(2,1)S(1)}, bf16[192,1024]{1,0:T(8,128)(2,1)S(1)}, u32[]{:S(2)}, u32[]{:S(2)}) collective-permute-start(bf16[192,1024]{1,0:T(8,128)(2,1)S(1)} %dynamic-slice_bitcast_fusion.10), channel_id=1, source_target_pairs={{0,8},{8,0},{16,24},{24,16},{1,9},{9,1},{17,25},{25,17},{2,10},{10... | collective-permute-start | bytes 1179656 | tf_op jit(solution)/shard_map/ppermute | solution.py:24
  196.0 16.0 %collective-permute-start.1 = (bf16[192,1024]{1,0:T(8,128)(2,1)S(1)}, bf16[192,1024]{1,0:T(8,128)(2,1)S(1)}, u32[]{:S(2)}, u32[]{:S(2)}) collective-permute-start(bf16[192,1024]{1,0:T(8,128)(2,1)S(1)} %dynamic-slice_bitcast_fusion.11), channel_id=1, source_target_pairs={{0,16},{8,24},{16,0},{24,8},{1,17},{9,25},{17,1},{25,9},{2,18},{10... | collective-permute-start | bytes 1179656 | tf_op jit(solution)/shard_map/ppermute | solution.py:24
  205.7 8.3 %copy-start.2 = (s32[128,4]{0,1:T(4,128)S(1)}, s32[128,4]{0,1:T(4,128)}, u32[]{:S(2)}) copy-start(s32[128,4]{0,1:T(4,128)} %param.10) | copy-start | bytes 6148
  211.8 4.7 %copy-start.1 = (bf16[1,768,2048]{2,1,0:T(8,128)(2,1)S(1)}, bf16[1,768,2048]{2,1,0:T(8,128)(2,1)}, u32[]{:S(2)}) copy-start(bf16[1,768,2048]{2,1,0:T(8,128)(2,1)} %param.13) | copy-start | bytes 9437188
Sparse Core Ops, SparseCore 0:
  9.6 49.8 all-gather.3
  61.1 45.9 all-gather.5
  131.4 51.2 reduce-scatter.1
